TPU v7x, 32 devices: a whole 2x2x4 slice. The times are simulated.
32 devices in a mesh: band: 8 (over z, y), member: 4 (over x, core).
Axes of the slice: x: 2, y: 2, z: 4, core: 2. Of those that a mesh axis runs over, the one named last changes fastest.
Arguments:
- targets: float32 [32, 64, 4096], P(('band', 'member')), may hold values from -6 to 6
- sources: float32 [16, 64, 4096], P('band', 'member'), may hold values from -6 to 6
Outputs:
- exchange: float32 [32, 64, 4096], P(('band', 'member'))
All inputs are finite; a program needn't handle non-finite values.
Results may differ from a plain program's by a relative error of at most 0.0003.
Values sent between devices are 32-bit elements; how exact they have to be, the bound alone decides.
No kernel may reach another device: no remote copies, remote signals or barrier semaphores. Data moves between devices by JAX's collectives and lax.ppermute only.
A program may use at most 64 MiB of HBM per device.

v0:
```python
import functools

import jax
import jax.numpy as jnp
import numpy as np
from jax import lax
from jax.experimental import pallas as pl
from jax.experimental.pallas import tpu as pltpu
from jax.sharding import PartitionSpec as P

STOPS = 2
LANES = 128

dot = functools.partial(jnp.dot, preferred_element_type=jnp.float32)


def cat(values, axis):
    return jnp.concatenate(values, axis=axis)


def split(values):
    high = values.astype(jnp.bfloat16)
    low = (values - high.astype(jnp.float32)).astype(jnp.bfloat16)
    return high, low


def tables(cells):
    wave = np.arange(cells) + 1.0
    sine = np.sin(np.pi * wave[:, None] * wave[None, :] / (cells + 1)).astype(np.float32)
    high = sine.astype(jnp.bfloat16)
    low = (sine - high.astype(np.float32)).astype(jnp.bfloat16)
    none = np.zeros_like(high)
    pair_high = np.block([[high, none], [none, high]])
    pair_low = np.block([[low, none], [none, low]])
    lane_table = np.block([[pair_high, pair_low], [pair_high, pair_low]])
    order = np.concatenate([np.arange(0, cells, 2), np.arange(1, cells, 2)])
    row_table = np.concatenate([high, high, low], 1)
    column_table = np.concatenate([high[:, order], high[:, order], low[:, order]], 1)
    back_table = np.concatenate([high[order], high[order], low[order]], 1)
    single = 4.0 * np.sin(np.pi * wave / (2.0 * (cells + 1))) ** 2
    eigen = single[:, None, None] + single[None, :, None] + single[None, None, :]
    inverse = (2.0 / (cells + 1)) ** 3 / eigen
    inverse = inverse.reshape(cells // 2, 2, cells, cells).transpose(0, 2, 1, 3)
    inverse = inverse.reshape(cells * cells // 2, 2 * cells).astype(np.float32)
    return lane_table, row_table, column_table, back_table, inverse


def solve_kernel(cells, parts, first, *refs):
    count = len(parts)
    pieces, refs = refs[:count], refs[count:]
    target, refs = refs[0], refs[1:]
    if not first:
        before, refs = refs[0], refs[1:]
    lane_table, row_table, column_table, back_table, inverse, out, source, planes, columns, sems = refs
    pairs = cells // 2
    plane_pitch, column_pitch = cells + 8, pairs + 8
    me = lax.axis_index("member")

    copies = []
    for number, (index, distance) in enumerate(parts):
        rows = pieces[number].shape[1]
        start = 0 if distance is None else pl.multiple_of((me ^ distance) * rows, 8)
        copy = pltpu.make_async_copy(pieces[number].at[index], source.at[pl.ds(start, rows), :], sems.at[number])
        copy.start()
        copies.append(copy)
    for copy in copies:
        copy.wait()

    low = lax.broadcasted_iota(jnp.int32, (pairs, LANES), 1) < cells

    def along_lanes(values):
        high, rest = split(values)
        product = dot(cat([high, rest], 1), lane_table[...])
        return product[:, :LANES] + product[:, LANES:]

    def along_rows(table, values):
        high, rest = split(values)
        return dot(table[...], cat([high, rest, high], 0))

    def tile(u):
        return slice(u * LANES, (u + 1) * LANES)

    def block(u):
        return slice(u * cells, (u + 1) * cells)

    field = along_lanes(cat([target[:, tile(u)] * source[:, tile(u)] for u in range(pairs)], 0))
    field = along_rows(row_table, cat([field[block(u)] for u in range(pairs)], 1))
    for u in range(pairs):
        planes[pl.ds(u * plane_pitch, cells), :] = field[:, tile(u)]

    turned = []
    for u in range(pairs):
        even = planes[pl.ds(2 * u, pairs, plane_pitch), :]
        odd = planes[pl.ds(2 * u + 1, pairs, plane_pitch), :]
        upper = jnp.where(low, even, pltpu.roll(odd, cells, 1))
        lower = jnp.where(low, pltpu.roll(even, cells, 1), odd)
        turned.append(cat([upper, lower], 0))
    field = along_rows(column_table, cat(turned, 1))
    field = field * cat([inverse[block(u), :] for u in range(pairs)], 1)
    field = along_rows(back_table, field)
    for u in range(pairs):
        upper, lower = field[:pairs, tile(u)], field[pairs:, tile(u)]
        columns[pl.ds(2 * u * column_pitch, pairs), :] = jnp.where(low, upper, pltpu.roll(lower, cells, 1))
        columns[pl.ds((2 * u + 1) * column_pitch, pairs), :] = jnp.where(low, pltpu.roll(upper, cells, 1), lower)

    field = along_rows(row_table, cat([columns[pl.ds(u, cells, column_pitch), :] for u in range(pairs)], 1))
    field = along_lanes(cat([field[:, tile(u)] for u in range(pairs)], 0))
    for u in range(pairs):
        term = source[:, tile(u)] * field[block(u)]
        out[:, tile(u)] = -term if first else before[:, tile(u)] - term


def solve(target, parts, total, constants):
    cells, plane = target.shape
    vmem = pl.BlockSpec(memory_space=pltpu.VMEM)
    anywhere = pl.BlockSpec(memory_space=pl.ANY)
    arrays = [part[0] for part in parts]
    layout = tuple(part[1:] for part in parts)
    operands = [target] + ([] if total is None else [total]) + list(constants)
    return pl.pallas_call(
        functools.partial(solve_kernel, cells, layout, total is None),
        out_shape=jax.ShapeDtypeStruct((cells, plane), jnp.float32),
        in_specs=[anywhere] * len(arrays) + [vmem] * len(operands),
        out_specs=vmem,
        scratch_shapes=[
            pltpu.VMEM((cells, plane), jnp.float32),
            pltpu.VMEM((cells // 2 * (cells + 8), LANES), jnp.float32),
            pltpu.VMEM((cells * (cells // 2 + 8), LANES), jnp.float32),
            pltpu.SemaphoreType.DMA((len(arrays),)),
        ],
        compiler_params=pltpu.CompilerParams(vmem_limit_bytes=24 << 20),
    )(*arrays, *operands)


def from_member(piece, distance):
    return lax.ppermute(piece, "member", [(i ^ distance, i) for i in range(lax.axis_size("member"))])


def from_band(piece):
    count = lax.axis_size("band")
    return lax.ppermute(piece, "band", [((i - 1) % count, i) for i in range(count)])


def body(targets, sources):
    cells = targets.shape[1]
    count = sources.shape[0]
    target = targets[0]
    constants = [jnp.asarray(table) for table in tables(cells)]
    total = None
    if lax.axis_size("member") != 4:
        slab = sources
        for stop in range(STOPS):
            if stop > 0:
                slab = from_band(slab)
            whole = lax.all_gather(slab, "member", axis=1, tiled=True)
            for index in range(count):
                total = solve(target, [(whole, index, None)], total, constants)
        return total[None]
    near = from_member(sources, 1)
    across = from_member(sources, 2)
    far = from_band(sources)
    far_across = from_member(far, 2)
    across_near = from_member(across, 1)
    far_near = from_member(far, 1)
    far_across_near = from_member(far_across, 1)
    for group in ((sources, near, across, across_near), (far, far_near, far_across, far_across_near)):
        for index in range(count):
            parts = [(piece, index, distance) for distance, piece in enumerate(group)]
            total = solve(target, parts, total, constants)
    return total[None]


def solution(mesh):
    placed = (P(("band", "member"), None, None), P("band", "member", None))
    return jax.shard_map(
        body,
        mesh=mesh,
        in_specs=placed,
        out_specs=P(("band", "member"), None, None),
        check_vma=False,
    )
```

profile of v0, /device:TPU:0, one launch (start us, length us, event | category | flops | bytes accessed | tf_op | source)
XLA Modules:
  0.0 50.7 jit_solution(9998084543261420448)
XLA Ops:
  0.0 3.0 %collective-permute-start = (f32[2,16,4096]{2,1,0:T(8,128)}, f32[2,16,4096]{2,1,0:T(8,128)S(1)}, u32[]{:S(2)}, u32[]{:S(2)}) collective-permute-start(f32[2,16,4096]{2,1,0:T(8,128)} %refs_0_.3), channel_id=1, source_target_pairs={{28,0},{0,4},{4,8},{8,12},{12,16},{16,20},{20,24},{24,28},{29,1},{... | collective-permute-start | bytes 1572872 | tf_op jit(solution)/shard_map/ppermute | solution.py:141
  3.0 1.5 %collective-permute-start.5 = (f32[2,16,4096]{2,1,0:T(8,128)}, f32[2,16,4096]{2,1,0:T(8,128)S(1)}, u32[]{:S(2)}, u32[]{:S(2)}) collective-permute-start(f32[2,16,4096]{2,1,0:T(8,128)} %refs_0_.3), channel_id=1, source_target_pairs={{2,0},{3,1},{0,2},{1,3},{6,4},{7,5},{4,6},{5,7},{10,8},{11,9},{8,1... | collective-permute-start | bytes 1572872 | tf_op jit(solution)/shard_map/ppermute | solution.py:136
  4.5 13.7 %collective-permute-done.refs_0_ = f32[2,16,4096]{2,1,0:T(8,128)S(1)} collective-permute-done((f32[2,16,4096]{2,1,0:T(8,128)}, f32[2,16,4096]{2,1,0:T(8,128)S(1)}, u32[]{:S(2)}, u32[]{:S(2)}) %collective-permute-start) | collective-permute-done | bytes 524320 | tf_op jit(solution)/shard_map/ppermute | solution.py:141
  18.1 1.5 %collective-permute-start.2 = (f32[2,16,4096]{2,1,0:T(8,128)S(1)}, f32[2,16,4096]{2,1,0:T(8,128)S(1)}, u32[]{:S(2)}, u32[]{:S(2)}) collective-permute-start(f32[2,16,4096]{2,1,0:T(8,128)S(1)} %collective-permute-done.refs_0_), channel_id=1, source_target_pairs={{2,0},{3,1},{0,2},{1,3},{6,4},{7,5},{4,6},{5,7},{10,8},{11,9},{8,1... | collective-permute-start | bytes 1572872 | tf_op jit(solution)/shard_map/ppermute | solution.py:136
  19.6 0.0 collective-permute-start.4
  19.6 0.0 collective-permute-done.5.refs_2_
  19.6 0.5 %collective-permute-start.6 = (f32[2,16,4096]{2,1,0:T(8,128)S(1)}, f32[2,16,4096]{2,1,0:T(8,128)S(1)}, u32[]{:S(2)}, u32[]{:S(2)}) collective-permute-start(f32[2,16,4096]{2,1,0:T(8,128)S(1)} %collective-permute-done.5.refs_2_), channel_id=1, source_target_pairs={{1,0},{0,1},{3,2},{2,3},{5,4},{4,5},{7,6},{6,7},{9,8},{8,9},{11,10... | collective-permute-start | bytes 1572872 | tf_op jit(solution)/shard_map/ppermute | solution.py:136
  20.1 0.0 collective-permute-start.1
  20.1 11.1 %collective-permute-done.2.refs_2_ = f32[2,16,4096]{2,1,0:T(8,128)S(1)} collective-permute-done((f32[2,16,4096]{2,1,0:T(8,128)S(1)}, f32[2,16,4096]{2,1,0:T(8,128)S(1)}, u32[]{:S(2)}, u32[]{:S(2)}) %collective-permute-start.2) | collective-permute-done | bytes 524320 | tf_op jit(solution)/shard_map/ppermute | solution.py:136
  31.2 0.0 collective-permute-start.3
  31.3 0.0 collective-permute-done.4.refs_1_
  31.3 0.0 collective-permute-done.6.refs_3_
  31.3 0.0 copy-start
  31.3 1.2 %copy-done = f32[1,64,4096]{2,1,0:T(8,128)S(1)} copy-done((f32[1,64,4096]{2,1,0:T(8,128)S(1)}, f32[1,64,4096]{2,1,0:T(8,128)}, u32[]{:S(2)}) %copy-start) | copy-done | bytes 1048600
  32.5 0.0 copy-start.2
  32.5 1.2 %copy-done.2 = f32[2048,128]{1,0:T(8,128)S(1)} copy-done((f32[2048,128]{1,0:T(8,128)S(1)}, f32[2048,128]{1,0:T(8,128)}, u32[]{:S(2)}) %copy-start.2) | copy-done | bytes 1048600
  33.7 0.0 copy-start.4
  33.7 0.9 %copy-done.4 = bf16[256,256]{1,0:T(8,128)(2,1)S(1)} copy-done((bf16[256,256]{1,0:T(8,128)(2,1)S(1)}, bf16[256,256]{1,0:T(8,128)(2,1)}, u32[]{:S(2)}) %copy-start.4) | copy-done | bytes 131096
  34.6 1.0 %copy-done.5 = f32[2,16,4096]{2,1,0:T(8,128)S(1)} copy-done((f32[2,16,4096]{2,1,0:T(8,128)S(1)}, f32[2,16,4096]{2,1,0:T(8,128)}, u32[]{:S(2)}) %copy-start.5) | copy-done | bytes 524312
  35.7 0.8 %copy-done.6 = bf16[64,192]{1,0:T(8,128)(2,1)S(1)} copy-done((bf16[64,192]{1,0:T(8,128)(2,1)S(1)}, bf16[64,192]{1,0:T(8,128)(2,1)}, u32[]{:S(2)}) %copy-start.6) | copy-done | bytes 24600
  36.4 0.8 %copy-done.7 = bf16[64,192]{1,0:T(8,128)(2,1)S(1)} copy-done((bf16[64,192]{1,0:T(8,128)(2,1)S(1)}, bf16[64,192]{1,0:T(8,128)(2,1)}, u32[]{:S(2)}) %copy-start.7) | copy-done | bytes 24600
  37.2 0.8 %copy-done.8 = bf16[64,192]{1,0:T(8,128)(2,1)S(1)} copy-done((bf16[64,192]{1,0:T(8,128)(2,1)S(1)}, bf16[64,192]{1,0:T(8,128)(2,1)}, u32[]{:S(2)}) %copy-start.8) | copy-done | bytes 24600
  37.9 2.9 %shard_map.73.refs_5_ = f32[64,4096]{1,0:T(8,128)S(1)} custom-call(f32[2,16,4096]{2,1,0:T(8,128)S(1)} %copy-done.5, f32[2,16,4096]{2,1,0:T(8,128)S(1)} %collective-permute-done.4.refs_1_, f32[2,16,4096]{2,1,0:T(8,128)S(1)} %collective-permute-done.5.refs_2_, f32[2,16,4096]{2,1,0:T(8,128)S(1)} %collective-permute-done.6.refs_3_, f32[64,4096]{1,0:T(8,128)S(1)} %bitcast.2, ...), custom_call_target="tpu_custom_call" | custom-call | tf_op jit(solution)/shard_map/pallas_call | solution.py:120
  40.9 0.0 copy-start.1
  40.9 0.0 copy-start.3
  40.9 2.9 %shard_map.74.refs_5_ = f32[64,4096]{1,0:T(8,128)S(1)} custom-call(f32[2,16,4096]{2,1,0:T(8,128)S(1)} %copy-done.5, f32[2,16,4096]{2,1,0:T(8,128)S(1)} %collective-permute-done.4.refs_1_, f32[2,16,4096]{2,1,0:T(8,128)S(1)} %collective-permute-done.5.refs_2_, f32[2,16,4096]{2,1,0:T(8,128)S(1)} %collective-permute-done.6.refs_3_, f32[64,4096]{1,0:T(8,128)S(1)} %bitcast.3, ...), custom_call_target="tpu_custom_call" | custom-call | tf_op jit(solution)/shard_map/pallas_call | solution.py:120
  43.8 0.0 collective-permute-done.1.refs_1_
  43.8 0.0 collective-permute-done.3.refs_3_
  43.9 0.0 copy-done.1
  43.9 0.0 copy-done.3
  43.9 2.9 %shard_map.75.refs_5_ = f32[64,4096]{1,0:T(8,128)S(1)} custom-call(f32[2,16,4096]{2,1,0:T(8,128)S(1)} %collective-permute-done.refs_0_, f32[2,16,4096]{2,1,0:T(8,128)S(1)} %collective-permute-done.1.refs_1_, f32[2,16,4096]{2,1,0:T(8,128)S(1)} %collective-permute-done.2.refs_2_, f32[2,16,4096]{2,1,0:T(8,128)S(1)} %collective-permute-done.3.refs_3_, ...), custom_call_target="tpu_custom_call" | custom-call | tf_op jit(solution)/shard_map/pallas_call | solution.py:120
  46.8 3.9 %shard_map.76 = f32[64,4096]{1,0:T(8,128)} custom-call(f32[2,16,4096]{2,1,0:T(8,128)S(1)} %collective-permute-done.refs_0_, f32[2,16,4096]{2,1,0:T(8,128)S(1)} %collective-permute-done.1.refs_1_, f32[2,16,4096]{2,1,0:T(8,128)S(1)} %collective-permute-done.2.refs_2_, f32[2,16,4096]{2,1,0:T(8,128)S(1)} %collective-permute-done.3.refs_3_, ...), custom_call_target="tpu_custom_call" | custom-call | tf_op jit(solution)/shard_map/pallas_call | solution.py:120
  (4 shorter events, 0.0 us)
Async XLA Ops:
  0.0 18.1 %collective-permute-start = (f32[2,16,4096]{2,1,0:T(8,128)}, f32[2,16,4096]{2,1,0:T(8,128)S(1)}, u32[]{:S(2)}, u32[]{:S(2)}) collective-permute-start(f32[2,16,4096]{2,1,0:T(8,128)} %refs_0_.3), channel_id=1, source_target_pairs={{28,0},{0,4},{4,8},{8,12},{12,16},{16,20},{20,24},{24,28},{29,1},{... | collective-permute-start | bytes 1572872 | tf_op jit(solution)/shard_map/ppermute | solution.py:141
  3.0 16.7 %collective-permute-start.5 = (f32[2,16,4096]{2,1,0:T(8,128)}, f32[2,16,4096]{2,1,0:T(8,128)S(1)}, u32[]{:S(2)}, u32[]{:S(2)}) collective-permute-start(f32[2,16,4096]{2,1,0:T(8,128)} %refs_0_.3), channel_id=1, source_target_pairs={{2,0},{3,1},{0,2},{1,3},{6,4},{7,5},{4,6},{5,7},{10,8},{11,9},{8,1... | collective-permute-start | bytes 1572872 | tf_op jit(solution)/shard_map/ppermute | solution.py:136
  18.1 13.1 %collective-permute-start.2 = (f32[2,16,4096]{2,1,0:T(8,128)S(1)}, f32[2,16,4096]{2,1,0:T(8,128)S(1)}, u32[]{:S(2)}, u32[]{:S(2)}) collective-permute-start(f32[2,16,4096]{2,1,0:T(8,128)S(1)} %collective-permute-done.refs_0_), channel_id=1, source_target_pairs={{2,0},{3,1},{0,2},{1,3},{6,4},{7,5},{4,6},{5,7},{10,8},{11,9},{8,1... | collective-permute-start | bytes 1572872 | tf_op jit(solution)/shard_map/ppermute | solution.py:136
  19.6 11.6 %collective-permute-start.4 = (f32[2,16,4096]{2,1,0:T(8,128)}, f32[2,16,4096]{2,1,0:T(8,128)S(1)}, u32[]{:S(2)}, u32[]{:S(2)}) collective-permute-start(f32[2,16,4096]{2,1,0:T(8,128)} %refs_0_.3), channel_id=1, source_target_pairs={{1,0},{0,1},{3,2},{2,3},{5,4},{4,5},{7,6},{6,7},{9,8},{8,9},{11,10... | collective-permute-start | bytes 1572872 | tf_op jit(solution)/shard_map/ppermute | solution.py:136
  19.6 11.6 %collective-permute-start.6 = (f32[2,16,4096]{2,1,0:T(8,128)S(1)}, f32[2,16,4096]{2,1,0:T(8,128)S(1)}, u32[]{:S(2)}, u32[]{:S(2)}) collective-permute-start(f32[2,16,4096]{2,1,0:T(8,128)S(1)} %collective-permute-done.5.refs_2_), channel_id=1, source_target_pairs={{1,0},{0,1},{3,2},{2,3},{5,4},{4,5},{7,6},{6,7},{9,8},{8,9},{11,10... | collective-permute-start | bytes 1572872 | tf_op jit(solution)/shard_map/ppermute | solution.py:136
  20.1 23.7 %collective-permute-start.1 = (f32[2,16,4096]{2,1,0:T(8,128)S(1)}, f32[2,16,4096]{2,1,0:T(8,128)S(1)}, u32[]{:S(2)}, u32[]{:S(2)}) collective-permute-start(f32[2,16,4096]{2,1,0:T(8,128)S(1)} %collective-permute-done.refs_0_), channel_id=1, source_target_pairs={{1,0},{0,1},{3,2},{2,3},{5,4},{4,5},{7,6},{6,7},{9,8},{8,9},{11,10... | collective-permute-start | bytes 1572872 | tf_op jit(solution)/shard_map/ppermute | solution.py:136
  31.2 12.6 %collective-permute-start.3 = (f32[2,16,4096]{2,1,0:T(8,128)S(1)}, f32[2,16,4096]{2,1,0:T(8,128)S(1)}, u32[]{:S(2)}, u32[]{:S(2)}) collective-permute-start(f32[2,16,4096]{2,1,0:T(8,128)S(1)} %collective-permute-done.2.refs_2_), channel_id=1, source_target_pairs={{1,0},{0,1},{3,2},{2,3},{5,4},{4,5},{7,6},{6,7},{9,8},{8,9},{11,10... | collective-permute-start | bytes 1572872 | tf_op jit(solution)/shard_map/ppermute | solution.py:136
  31.3 1.2 %copy-start = (f32[1,64,4096]{2,1,0:T(8,128)S(1)}, f32[1,64,4096]{2,1,0:T(8,128)}, u32[]{:S(2)}) copy-start(f32[1,64,4096]{2,1,0:T(8,128)} %param.7) | copy-start | bytes 3145732
  32.5 1.2 %copy-start.2 = (f32[2048,128]{1,0:T(8,128)S(1)}, f32[2048,128]{1,0:T(8,128)}, u32[]{:S(2)}) copy-start(f32[2048,128]{1,0:T(8,128)} %constant.14.clone.refs_9_.refs_10_) | copy-start | bytes 3145732
  33.7 0.9 %copy-start.4 = (bf16[256,256]{1,0:T(8,128)(2,1)S(1)}, bf16[256,256]{1,0:T(8,128)(2,1)}, u32[]{:S(2)}) copy-start(bf16[256,256]{1,0:T(8,128)(2,1)} %constant.10.clone.refs_5_.refs_6_) | copy-start | bytes 393220
  34.6 1.0 %copy-start.5 = (f32[2,16,4096]{2,1,0:T(8,128)S(1)}, f32[2,16,4096]{2,1,0:T(8,128)}, u32[]{:S(2)}) copy-start(f32[2,16,4096]{2,1,0:T(8,128)} %refs_0_.3) | copy-start | bytes 1572868
  35.7 0.8 %copy-start.6 = (bf16[64,192]{1,0:T(8,128)(2,1)S(1)}, bf16[64,192]{1,0:T(8,128)(2,1)}, u32[]{:S(2)}) copy-start(bf16[64,192]{1,0:T(8,128)(2,1)} %constant.11.clone.refs_6_.refs_7_) | copy-start | bytes 73732
  36.4 0.8 %copy-start.7 = (bf16[64,192]{1,0:T(8,128)(2,1)S(1)}, bf16[64,192]{1,0:T(8,128)(2,1)}, u32[]{:S(2)}) copy-start(bf16[64,192]{1,0:T(8,128)(2,1)} %constant.12.clone.refs_7_.refs_8_) | copy-start | bytes 73732
  37.2 0.8 %copy-start.8 = (bf16[64,192]{1,0:T(8,128)(2,1)S(1)}, bf16[64,192]{1,0:T(8,128)(2,1)}, u32[]{:S(2)}) copy-start(bf16[64,192]{1,0:T(8,128)(2,1)} %constant.13.clone.refs_8_.refs_9_) | copy-start | bytes 73732
  40.9 3.0 %copy-start.1 = (f32[1,64,4096]{2,1,0:T(8,128)S(1)}, f32[1,64,4096]{2,1,0:T(8,128)}, u32[]{:S(2)}) copy-start(f32[1,64,4096]{2,1,0:T(8,128)} %param.7) | copy-start | bytes 3145732
  40.9 3.0 %copy-start.3 = (f32[2048,128]{1,0:T(8,128)S(1)}, f32[2048,128]{1,0:T(8,128)}, u32[]{:S(2)}) copy-start(f32[2048,128]{1,0:T(8,128)} %constant.14.clone.refs_9_.refs_10_) | copy-start | bytes 3145732
where the time goes:
time: 51.2 us; the launch traced here: 50.7 us
  waiting for transfers between devices  24.8 us (48%)
  Pallas kernels  12.7 us (25%)
  local copies, waits for them, and re-layouts  6.67 us (13%)
  starting transfers between devices  6.47 us (13%)
    ppermute x1, waiting for transfers between devices, from_band(): lax.ppermute(piece, 'band', [((i - 1) % count, i) for i in range(count)])  13.7 us
    pallas_call x4, Pallas kernels, solve(): pl.pallas_call(functools.partial(solve_kernel, cells, layout, total is No...  12.7 us
    ppermute x6, waiting for transfers between devices, from_member(): lax.ppermute(piece, 'member', [(i ^ distance, i) for i in range(lax.axis_...  11.1 us
    unnamed x18, local copies, waits for them, and re-layouts  6.67 us
    ppermute x6, starting transfers between devices, from_member(): lax.ppermute(piece, 'member', [(i ^ distance, i) for i in range(lax.axis_...  3.5 us
    ppermute x1, starting transfers between devices, from_band(): lax.ppermute(piece, 'band', [((i - 1) % count, i) for i in range(count)])  2.97 us
  transfers between devices with their start and end apart: 7, of which 2 were waited for; matrix products, arithmetic and copies ran while one was open for 0% of the time, Pallas kernels for 12%

commit v1 on v0

v1 whole, which is shorter than its diff:
```python
import functools

import jax
import jax.numpy as jnp
import numpy as np
from jax import lax
from jax.experimental import pallas as pl
from jax.experimental.pallas import tpu as pltpu
from jax.sharding import PartitionSpec as P

STOPS = 2
LANES = 128
ROWS = 8
CHUNKS = 2

dot = functools.partial(jnp.dot, preferred_element_type=jnp.float32)


def cat(values, axis):
    return jnp.concatenate(values, axis=axis)


def split(values):
    high = values.astype(jnp.bfloat16)
    low = (values - high.astype(jnp.float32)).astype(jnp.bfloat16)
    return high, low


def tables(cells, layouts):
    wave = np.arange(cells) + 1.0
    sine = np.sin(np.pi * wave[:, None] * wave[None, :] / (cells + 1)).astype(np.float32)
    high = sine.astype(jnp.bfloat16)
    low = (sine - high.astype(np.float32)).astype(jnp.bfloat16)
    none = np.zeros_like(high)
    pair_high = np.block([[high, none], [none, high]])
    pair_low = np.block([[low, none], [none, low]])
    lane_table = np.block([[pair_high, pair_low], [pair_high, pair_low]])
    order = np.concatenate([np.arange(0, cells, 2), np.arange(1, cells, 2)])
    plane_table = np.stack([np.concatenate([high[:, rows], high[:, rows], low[:, rows]], 1) for rows in layouts])
    plane_back_table = np.stack([np.concatenate([high[rows], high[rows], low[rows]], 1) for rows in layouts])
    column_table = np.concatenate([high[:, order], high[:, order], low[:, order]], 1)
    back_table = np.concatenate([high[order], high[order], low[order]], 1)
    single = 4.0 * np.sin(np.pi * wave / (2.0 * (cells + 1))) ** 2
    eigen = single[:, None, None] + single[None, :, None] + single[None, None, :]
    inverse = (2.0 / (cells + 1)) ** 3 / eigen
    inverse = inverse.reshape(cells // 2, 2, cells, cells).transpose(0, 2, 1, 3)
    inverse = inverse.reshape(cells * cells // 2, 2 * cells).astype(np.float32)
    return lane_table, plane_table, plane_back_table, column_table, back_table, inverse


def prepare_kernel(count, *refs):
    outs, sems = refs[-count - 1:-1], refs[-1]
    copies = [pltpu.make_async_copy(refs[i], outs[i], sems.at[i]) for i in range(count)]
    for copy in copies:
        copy.start()
    for copy in copies:
        copy.wait()


def in_vmem(arrays, *earlier):
    return pl.pallas_call(
        functools.partial(prepare_kernel, len(arrays)),
        out_shape=[pltpu.VMEM(array.shape, array.dtype) for array in arrays],
        in_specs=[pl.BlockSpec(memory_space=pltpu.HBM)] * len(arrays) + [pl.BlockSpec(memory_space=pl.ANY)] * len(earlier),
        out_specs=[pl.BlockSpec(memory_space=pltpu.VMEM)] * len(arrays),
        scratch_shapes=[pltpu.SemaphoreType.DMA((len(arrays),))],
        compiler_params=pltpu.CompilerParams(vmem_limit_bytes=1 << 20),
    )(*[pltpu.with_memory_space_constraint(array, pltpu.HBM) for array in arrays], *earlier)


def parts_kernel(source, *refs):
    outs, sems = refs[:-1], refs[-1]
    copies = [pltpu.make_async_copy(source.at[pl.ds(i, 1)], out, sems.at[i]) for i, out in enumerate(outs)]
    for copy in copies:
        copy.start()
    for copy in copies:
        copy.wait()


def in_vmem_parts(sources):
    count, extent, plane = sources.shape
    return pl.pallas_call(
        parts_kernel,
        out_shape=[pltpu.VMEM((1, extent, plane), sources.dtype)] * count,
        in_specs=[pl.BlockSpec(memory_space=pltpu.HBM)],
        out_specs=[pl.BlockSpec(memory_space=pltpu.VMEM)] * count,
        scratch_shapes=[pltpu.SemaphoreType.DMA((count,))],
        compiler_params=pltpu.CompilerParams(vmem_limit_bytes=1 << 20),
    )(pltpu.with_memory_space_constraint(sources, pltpu.HBM))


def parts_kernel(source, *refs):
    outs, sems = refs[:-1], refs[-1]
    copies = [pltpu.make_async_copy(source.at[pl.ds(i, 1)], out, sems.at[i]) for i, out in enumerate(outs)]
    for copy in copies:
        copy.start()
    for copy in copies:
        copy.wait()


def in_vmem_parts(sources):
    count, extent, plane = sources.shape
    return pl.pallas_call(
        parts_kernel,
        out_shape=[pltpu.VMEM((1, extent, plane), sources.dtype)] * count,
        in_specs=[pl.BlockSpec(memory_space=pltpu.HBM)],
        out_specs=[pl.BlockSpec(memory_space=pltpu.VMEM)] * count,
        scratch_shapes=[pltpu.SemaphoreType.DMA((count,))],
        compiler_params=pltpu.CompilerParams(vmem_limit_bytes=1 << 20),
    )(pltpu.with_memory_space_constraint(sources, pltpu.HBM))


def solve_kernel(cells, groups, spare, first, last, *refs):
    sources = len(groups)
    pieces = []
    for group in groups:
        pieces.append(refs[:len(group)])
        refs = refs[len(group):]
    refs = refs[spare:]
    target, refs = refs[0], refs[1:]
    if not first:
        before, refs = refs[0], refs[1:]
    lane_table, plane_table, plane_back_table, column_table, back_table, inverse, out, planes, columns = refs[:9]
    pairs = cells // 2
    plane_pitch, column_pitch = cells + 8, pairs + 8
    me = lax.axis_index("member")
    extent = cells // lax.axis_size("member")
    places = [
        [(number, index, row) for number, (index, _, _, count) in enumerate(group) for row in range(0, count, ROWS)]
        for group in groups
    ]
    layout = [
        (distance, offset + row) for _, distance, offset, count in groups[0] for row in range(0, count, ROWS)
    ]

    def rows(segment):
        distance, offset = layout[segment]
        start = offset if distance is None else (me ^ distance) * extent + offset
        return pl.ds(pl.multiple_of(start, ROWS), ROWS)

    order = 0 if layout[0][0] is None else me
    low = lax.broadcasted_iota(jnp.int32, (pairs, LANES), 1) < cells
    every = [(j, u) for j in range(sources) for u in range(pairs)]

    def along_lanes(values):
        high, rest = split(values)
        product = dot(cat([high, rest], 1), lane_table[...])
        return product[:, :LANES] + product[:, LANES:]

    def along_rows(table, values):
        high, rest = split(values)
        return dot(table, cat([high, rest, high], 0))

    def tile(u):
        return slice(u * LANES, (u + 1) * LANES)

    def block(u):
        return slice(u * cells, (u + 1) * cells)

    def piece(j, segment, u):
        number, index, row = places[j][segment]
        return pieces[j][number][index, row:row + ROWS, tile(u)]

    segments = range(len(layout))
    field = [target[rows(segment), tile(u)] * piece(j, segment, u) for j, u in every for segment in segments]
    field = along_lanes(cat(field, 0))
    field = along_rows(plane_table[order], cat([field[block(i)] for i in range(len(every))], 1))
    for i, (j, u) in enumerate(every):
        planes[j, pl.ds(u * plane_pitch, cells), :] = field[:, tile(i)]

    turned = []
    for j, u in every:
        even = planes[j, pl.ds(2 * u, pairs, plane_pitch), :]
        odd = planes[j, pl.ds(2 * u + 1, pairs, plane_pitch), :]
        upper = jnp.where(low, even, pltpu.roll(odd, cells, 1))
        lower = jnp.where(low, pltpu.roll(even, cells, 1), odd)
        turned.append(cat([upper, lower], 0))
    field = along_rows(column_table[...], cat(turned, 1))
    field = field * cat([inverse[block(u), :] for _, u in every], 1)
    field = along_rows(back_table[...], field)
    for i, (j, u) in enumerate(every):
        upper, lower = field[:pairs, tile(i)], field[pairs:, tile(i)]
        columns[j, pl.ds(2 * u * column_pitch, pairs), :] = jnp.where(low, upper, pltpu.roll(lower, cells, 1))
        columns[j, pl.ds((2 * u + 1) * column_pitch, pairs), :] = jnp.where(low, pltpu.roll(upper, cells, 1), lower)

    parted = CHUNKS if last else 1
    copies = []
    for chunk in range(parted):
        mine = range(chunk * pairs // parted, (chunk + 1) * pairs // parted)
        some = [(j, u) for j in range(sources) for u in mine]
        field = cat([columns[j, pl.ds(u, cells, column_pitch), :] for j, u in some], 1)
        field = along_rows(plane_back_table[order], field)
        field = along_lanes(cat([field[:, tile(i)] for i in range(len(some))], 0))
        result = refs[9] if last else out
        for position, u in enumerate(mine):
            for segment in segments:
                value = 0.0 if first else before[rows(segment), tile(u)]
                for j in range(sources):
                    start = (j * len(mine) + position) * cells + segment * ROWS
                    value = value - piece(j, segment, u) * field[start:start + ROWS]
                result[rows(segment), tile(u)] = value
        if last:
            span = pl.ds(mine[0] * LANES, len(mine) * LANES)
            copy = pltpu.make_async_copy(result.at[:, span], out.at[:, span], refs[10].at[chunk])
            copy.start()
            copies.append(copy)
    for copy in copies:
        copy.wait()


def solve(target, groups, total, constants, last, *earlier):
    cells, plane = target.shape
    vmem = pl.BlockSpec(memory_space=pltpu.VMEM)
    layout = tuple(tuple(part[1:] for part in group) for group in groups)
    operands = [part[0] for group in groups for part in group]
    operands += list(earlier) + [target] + ([] if total is None else [total]) + list(constants)
    operands = [pltpu.with_memory_space_constraint(operand, pltpu.VMEM) for operand in operands]
    shape = (cells, plane)
    scratch = [
        pltpu.VMEM((len(groups), cells // 2 * (cells + 8), LANES), jnp.float32),
        pltpu.VMEM((len(groups), cells * (cells // 2 + 8), LANES), jnp.float32),
    ]
    if last:
        scratch += [pltpu.VMEM(shape, jnp.float32), pltpu.SemaphoreType.DMA((CHUNKS,))]
    return pl.pallas_call(
        functools.partial(solve_kernel, cells, layout, len(earlier), total is None, last),
        out_shape=jax.ShapeDtypeStruct(shape, jnp.float32) if last else pltpu.VMEM(shape, jnp.float32),
        in_specs=[vmem] * len(operands),
        out_specs=pl.BlockSpec(memory_space=pltpu.HBM if last else pltpu.VMEM),
        scratch_shapes=scratch,
        compiler_params=pltpu.CompilerParams(vmem_limit_bytes=32 << 20),
    )(*operands)


def from_member(piece, distance):
    return lax.ppermute(piece, "member", [(i ^ distance, i) for i in range(lax.axis_size("member"))])


def from_band(piece):
    count = lax.axis_size("band")
    return lax.ppermute(piece, "band", [((i - 1) % count, i) for i in range(count)])


def after(value, *earlier):
    return lax.optimization_barrier((value, *earlier))[0]


def body(targets, sources):
    cells = targets.shape[1]
    count, extent = sources.shape[:2]
    members = lax.axis_size("member")
    if members != 4:
        constants = in_vmem([targets[0]] + [jnp.asarray(table) for table in tables(cells, [np.arange(cells)])])
        total = None
        slab = sources
        for stop in range(STOPS):
            if stop > 0:
                slab = from_band(slab)
            whole = lax.all_gather(slab, "member", axis=1, tiled=True)
            for index in range(count):
                last = stop == STOPS - 1 and index == count - 1
                total = solve(constants[0], [[(whole, index, None, 0, cells)]], total, constants[1:], last)
        return total[None]
    member_rows = np.arange(cells).reshape(members, extent)
    layouts = [np.concatenate([member_rows[i ^ k] for k in range(members)]) for i in range(members)]
    everything = [jnp.asarray(table) for table in tables(cells, layouts)]
    mine = in_vmem_parts(sources)
    across, far = [None, None], [None, None]
    across[0] = from_member(mine[0], 2)
    far[1] = from_band(mine[1])
    across[1] = from_member(mine[1], 2)
    near = from_member(sources, 1)
    far[0] = from_band(after(mine[0], near))
    target, *constants = in_vmem([targets[0]] + everything, near)
    across[0], far[1] = after(across[0], target), after(far[1], target)
    far_across = [from_band(across[0]), from_member(far[1], 2)]
    half = extent // 2
    across_near = [[from_member(across[0], 1)], None]
    late = after(across[1], across_near[0][0], far[0])
    across_near[1] = [from_member(late[:, i * half:(i + 1) * half], 1) for i in range(2)]
    groups = [[(mine[i], 0, 0, 0, extent), (near, i, 1, 0, extent), (across[i], 0, 2, 0, extent)] for i in range(2)]
    groups[0] += [(across_near[0][0], 0, 3, 0, extent)]
    groups[1] += [(across_near[1][i], 0, 3, i * half, half) for i in range(2)]
    total = solve(target, groups, None, constants, False, far[0])
    far_near = [from_member(value, 1) for value in far]
    far_across = [after(value, total) for value in far_across]
    far_across_near = [from_member(value, 1) for value in far_across]
    groups = [[(far[i], 0, 0), (far_near[i], 0, 1), (far_across[i], 0, 2), (far_across_near[i], 0, 3)] for i in range(2)]
    groups = [[part + (0, extent) for part in group] for group in groups]
    total = solve(target, groups, total, constants, True)
    return total[None]


def solution(mesh):
    placed = (P(("band", "member"), None, None), P("band", "member", None))
    return jax.shard_map(
        body,
        mesh=mesh,
        in_specs=placed,
        out_specs=P(("band", "member"), None, None),
        check_vma=False,
    )
```

time: 51.2 us -> 34.4 us (0.67)
  waiting for transfers between devices: 24.8 us -> 12 us
  local copies, waits for them, and re-layouts: 6.67 us -> 0.02 us
  starting transfers between devices: 6.47 us -> 10.3 us
  Pallas kernels: 12.7 us -> 11.9 us
    unnamed x18 -> x0, local copies, waits for them, and re-layouts: 6.67 us -> none
    ppermute x6 -> x11, waiting for transfers between devices: 11.1 us -> 4.44 us  [from_member(): lax.ppermute(piece, 'member', [(i ^ distance, i) for i in range(lax.axis_...]
    ppermute x1 -> x3, waiting for transfers between devices: 13.7 us -> 7.54 us  [from_band(): lax.ppermute(piece, 'band', [((i - 1) % count, i) for i in range(count)])]
    ppermute x1 -> x3, starting transfers between devices: 2.97 us -> 5.01 us  [from_band(): lax.ppermute(piece, 'band', [((i - 1) % count, i) for i in range(count)])]
    ppermute x6 -> x11, starting transfers between devices: 3.5 us -> 5.26 us  [from_member(): lax.ppermute(piece, 'member', [(i ^ distance, i) for i in range(lax.axis_...]
    pallas_call x4, Pallas kernels: 12.7 us -> 11.9 us  [the longest x2 9.09 us: solve(): pl.pallas_call(functools.partial(solve_kernel, cells, layout, len(earlier...]
  transfers between devices with their start and end apart: 7 -> 14, of which waited for: 2 -> 7; matrix products, arithmetic and copies ran while one was open for 0% -> 0% of each run, Pallas kernels for 12% -> 20%
where the time goes in v1:
time: 34.4 us; the launch traced here: 34.2 us
  waiting for transfers between devices  12 us (35%)
  Pallas kernels  11.9 us (35%)
  starting transfers between devices  10.3 us (30%)
    pallas_call x2, Pallas kernels, solve(): pl.pallas_call(functools.partial(solve_kernel, cells, layout, len(earlier...  9.09 us
    ppermute x3, waiting for transfers between devices, from_band(): lax.ppermute(piece, 'band', [((i - 1) % count, i) for i in range(count)])  7.54 us
    ppermute x11, starting transfers between devices, from_member(): lax.ppermute(piece, 'member', [(i ^ distance, i) for i in range(lax.axis_...  5.26 us
    ppermute x3, starting transfers between devices, from_band(): lax.ppermute(piece, 'band', [((i - 1) % count, i) for i in range(count)])  5.01 us
    ppermute x11, waiting for transfers between devices, from_member(): lax.ppermute(piece, 'member', [(i ^ distance, i) for i in range(lax.axis_...  4.44 us
    pallas_call x1, Pallas kernels, in_vmem(): pl.pallas_call(functools.partial(prepare_kernel, len(arrays)), out_shape=...  1.75 us
    pallas_call x1, Pallas kernels, in_vmem_parts(): pl.pallas_call(parts_kernel, out_shape=[pltpu.VMEM((1, extent, plane), so...  1.04 us
  transfers between devices with their start and end apart: 14, of which 7 were waited for; matrix products, arithmetic and copies ran while one was open for 0% of the time, Pallas kernels for 20%

profile of v1, /device:TPU:0, one launch (start us, length us, event | category | flops | bytes accessed | tf_op | source)
XLA Modules:
  0.0 34.2 jit_solution(693271437697791813)
XLA Ops:
  0.0 0.5 %collective-permute-start = (f32[2,16,4096]{2,1,0:T(8,128)}, f32[2,16,4096]{2,1,0:T(8,128)S(1)}, u32[]{:S(2)}, u32[]{:S(2)}) collective-permute-start(f32[2,16,4096]{2,1,0:T(8,128)} %source.1), channel_id=1, source_target_pairs={{1,0},{0,1},{3,2},{2,3},{5,4},{4,5},{7,6},{6,7},{9,8},{8,9},{11,10... | collective-permute-start | bytes 1572872 | tf_op jit(solution)/shard_map/ppermute | solution.py:236
  0.5 1.0 %shard_map.82 = (f32[1,16,4096]{2,1,0:T(8,128)S(1)}, f32[1,16,4096]{2,1,0:T(8,128)S(1)}) custom-call(f32[2,16,4096]{2,1,0:T(8,128)} %source.1), custom_call_target="tpu_custom_call" | custom-call | tf_op jit(solution)/shard_map/pallas_call | solution.py:103
  1.5 2.6 %collective-permute-start.3 = (f32[1,16,4096]{2,1,0:T(8,128)S(1)}, f32[1,16,4096]{2,1,0:T(8,128)S(1)}, u32[]{:S(2)}, u32[]{:S(2)}) collective-permute-start(f32[1,16,4096]{2,1,0:T(8,128)S(1)} %get-tuple-element.21.refs_0_), channel_id=1, source_target_pairs={{2,0},{3,1},{0,2},{1,3},{6,4},{7,5},{4,6},{5,7},{10,8},{11,9},{8,1... | collective-permute-start | bytes 786440 | tf_op jit(solution)/shard_map/ppermute | solution.py:236
  4.1 1.5 %collective-permute-start.10 = (f32[1,16,4096]{2,1,0:T(8,128)S(1)}, f32[1,16,4096]{2,1,0:T(8,128)S(1)}, u32[]{:S(2)}, u32[]{:S(2)}) collective-permute-start(f32[1,16,4096]{2,1,0:T(8,128)S(1)} %get-tuple-element.24.refs_4_), channel_id=1, source_target_pairs={{28,0},{0,4},{4,8},{8,12},{12,16},{16,20},{20,24},{24,28},{29,1},{... | collective-permute-start | bytes 786440 | tf_op jit(solution)/shard_map/ppermute | solution.py:241
  5.6 0.5 %collective-permute-start.6 = (f32[1,16,4096]{2,1,0:T(8,128)S(1)}, f32[1,16,4096]{2,1,0:T(8,128)S(1)}, u32[]{:S(2)}, u32[]{:S(2)}) collective-permute-start(f32[1,16,4096]{2,1,0:T(8,128)S(1)} %get-tuple-element.24.refs_4_), channel_id=1, source_target_pairs={{2,0},{3,1},{0,2},{1,3},{6,4},{7,5},{4,6},{5,7},{10,8},{11,9},{8,1... | collective-permute-start | bytes 786440 | tf_op jit(solution)/shard_map/ppermute | solution.py:236
  6.1 0.0 collective-permute-done.refs_7_.refs_1_.refs_5_
  6.1 1.5 %collective-permute-start.1 = (f32[1,16,4096]{2,1,0:T(8,128)S(1)}, f32[1,16,4096]{2,1,0:T(8,128)S(1)}, u32[]{:S(2)}, u32[]{:S(2)}) collective-permute-start(f32[1,16,4096]{2,1,0:T(8,128)S(1)} %get-tuple-element.21.refs_0_), channel_id=1, source_target_pairs={{28,0},{0,4},{4,8},{8,12},{12,16},{16,20},{20,24},{24,28},{29,1},{... | collective-permute-start | bytes 786440 | tf_op jit(solution)/shard_map/ppermute | solution.py:241
  7.6 1.8 %shard_map.83 = (f32[64,4096]{1,0:T(8,128)S(1)}, bf16[256,256]{1,0:T(8,128)(2,1)S(1)}, bf16[4,64,192]{2,1,0:T(8,128)(2,1)S(1)}, bf16[4,64,192]{2,1,0:T(8,128)(2,...) custom-call(f32[64,4096]{1,0:T(8,128)} %bitcast.2, ...), custom_call_target="tpu_custom_call" | custom-call | tf_op jit(solution)/shard_map/pallas_call | solution.py:61
  9.4 1.8 %collective-permute-done.3.refs_2_ = f32[1,16,4096]{2,1,0:T(8,128)S(1)} collective-permute-done((f32[1,16,4096]{2,1,0:T(8,128)S(1)}, f32[1,16,4096]{2,1,0:T(8,128)S(1)}, u32[]{:S(2)}, u32[]{:S(2)}) %collective-permute-start.3) | collective-permute-done | bytes 262176 | tf_op jit(solution)/shard_map/ppermute | solution.py:236
  11.2 0.0 collective-permute-start.5
  11.2 2.0 %collective-permute-start.4 = (f32[1,16,4096]{2,1,0:T(8,128)S(1)}, f32[1,16,4096]{2,1,0:T(8,128)S(1)}, u32[]{:S(2)}, u32[]{:S(2)}) collective-permute-start(f32[1,16,4096]{2,1,0:T(8,128)S(1)} %collective-permute-done.3.refs_2_), channel_id=1, source_target_pairs={{28,0},{0,4},{4,8},{8,12},{12,16},{16,20},{20,24},{24,28},{29,1},{... | collective-permute-start | bytes 786440 | tf_op jit(solution)/shard_map/ppermute | solution.py:241
  13.2 2.7 %collective-permute-done.10.refs_4_ = f32[1,16,4096]{2,1,0:T(8,128)S(1)} collective-permute-done((f32[1,16,4096]{2,1,0:T(8,128)S(1)}, f32[1,16,4096]{2,1,0:T(8,128)S(1)}, u32[]{:S(2)}, u32[]{:S(2)}) %collective-permute-start.10) | collective-permute-done | bytes 262176 | tf_op jit(solution)/shard_map/ppermute | solution.py:241
  15.9 0.3 %collective-permute-start.12 = (f32[1,16,4096]{2,1,0:T(8,128)S(1)}, f32[1,16,4096]{2,1,0:T(8,128)S(1)}, u32[]{:S(2)}, u32[]{:S(2)}) collective-permute-start(f32[1,16,4096]{2,1,0:T(8,128)S(1)} %collective-permute-done.10.refs_4_), channel_id=1, source_target_pairs={{2,0},{3,1},{0,2},{1,3},{6,4},{7,5},{4,6},{5,7},{10,8},{11,9},{8,1... | collective-permute-start | bytes 786440 | tf_op jit(solution)/shard_map/ppermute | solution.py:236
  16.2 0.4 %collective-permute-done.6.refs_6_ = f32[1,16,4096]{2,1,0:T(8,128)S(1)} collective-permute-done((f32[1,16,4096]{2,1,0:T(8,128)S(1)}, f32[1,16,4096]{2,1,0:T(8,128)S(1)}, u32[]{:S(2)}, u32[]{:S(2)}) %collective-permute-start.6) | collective-permute-done | bytes 262176 | tf_op jit(solution)/shard_map/ppermute | solution.py:236
  16.7 4.8 %collective-permute-done.1.refs_9_.refs_0_ = f32[1,16,4096]{2,1,0:T(8,128)S(1)} collective-permute-done((f32[1,16,4096]{2,1,0:T(8,128)S(1)}, f32[1,16,4096]{2,1,0:T(8,128)S(1)}, u32[]{:S(2)}, u32[]{:S(2)}) %collective-permute-start.1) | collective-permute-done | bytes 262176 | tf_op jit(solution)/shard_map/ppermute | solution.py:241
  21.5 0.0 collective-permute-done.5.refs_3_
  21.5 0.1 collective-permute-start.8
  21.6 0.5 %collective-permute-start.7 = (f32[1,8,4096]{2,1,0:T(8,128)S(1)}, f32[1,8,4096]{2,1,0:T(8,128)S(1)}, u32[]{:S(2)}, u32[]{:S(2)}) collective-permute-start(f32[1,8,4096]{2,1,0:T(8,128)S(1)} %get-tuple-element.36), channel_id=1, source_target_pairs={{1,0},{0,1},{3,2},{2,3},{5,4},{4,5},{7,6},{6,7},{9,8},{8,9},{11,10... | collective-permute-start | bytes 393224 | tf_op jit(solution)/shard_map/ppermute | solution.py:236
  22.1 0.1 collective-permute-start.11
  22.2 0.8 %collective-permute-done.8.refs_8_ = f32[1,8,4096]{2,1,0:T(8,128)S(1)} collective-permute-done((f32[1,8,4096]{2,1,0:T(8,128)S(1)}, f32[1,8,4096]{2,1,0:T(8,128)S(1)}, u32[]{:S(2)}, u32[]{:S(2)}) %collective-permute-start.8) | collective-permute-done | bytes 131104 | tf_op jit(solution)/shard_map/ppermute | solution.py:236
  22.9 0.1 collective-permute-start.2
  23.1 0.0 collective-permute-done.7.refs_7_
  23.1 4.1 %shard_map.84.refs_9_ = f32[64,4096]{1,0:T(8,128)S(1)} custom-call(f32[1,16,4096]{2,1,0:T(8,128)S(1)} %get-tuple-element.21.refs_0_, f32[2,16,4096]{2,1,0:T(8,128)S(1)} %collective-permute-done.refs_7_.refs_1_.refs_5_, f32[1,16,4096]{2,1,0:T(8,128)S(1)} %collective-permute-done.3.refs_2_, f32[1,16,4096]{2,1,0:T(8,128)S(1)} %collective-permute-done.5.refs_3_, ...), custom_call_target="tpu_custom_call" | custom-call | tf_op jit(solution)/shard_map/pallas_call | solution.py:225
  27.3 0.0 collective-permute-done.4.refs_2_
  27.3 0.4 %collective-permute-start.9 = (f32[1,16,4096]{2,1,0:T(8,128)S(1)}, f32[1,16,4096]{2,1,0:T(8,128)S(1)}, u32[]{:S(2)}, u32[]{:S(2)}) collective-permute-start(f32[1,16,4096]{2,1,0:T(8,128)S(1)} %collective-permute-done.4.refs_2_), channel_id=1, source_target_pairs={{1,0},{0,1},{3,2},{2,3},{5,4},{4,5},{7,6},{6,7},{9,8},{8,9},{11,10... | collective-permute-start | bytes 786440 | tf_op jit(solution)/shard_map/ppermute | solution.py:236
  27.7 0.0 collective-permute-done.12.refs_6_
  27.7 0.2 collective-permute-start.13
  27.9 0.0 collective-permute-done.11.refs_5_
  27.9 0.0 collective-permute-done.2.refs_1_
  27.9 1.0 %collective-permute-done.9.refs_3_ = f32[1,16,4096]{2,1,0:T(8,128)S(1)} collective-permute-done((f32[1,16,4096]{2,1,0:T(8,128)S(1)}, f32[1,16,4096]{2,1,0:T(8,128)S(1)}, u32[]{:S(2)}, u32[]{:S(2)}) %collective-permute-start.9) | collective-permute-done | bytes 262176 | tf_op jit(solution)/shard_map/ppermute | solution.py:236
  28.9 0.4 %collective-permute-done.13.refs_7_ = f32[1,16,4096]{2,1,0:T(8,128)S(1)} collective-permute-done((f32[1,16,4096]{2,1,0:T(8,128)S(1)}, f32[1,16,4096]{2,1,0:T(8,128)S(1)}, u32[]{:S(2)}, u32[]{:S(2)}) %collective-permute-start.13) | collective-permute-done | bytes 262176 | tf_op jit(solution)/shard_map/ppermute | solution.py:236
  29.3 4.9 %shard_map.85 = f32[64,4096]{1,0:T(8,128)} custom-call(f32[1,16,4096]{2,1,0:T(8,128)S(1)} %collective-permute-done.1.refs_9_.refs_0_, f32[1,16,4096]{2,1,0:T(8,128)S(1)} %collective-permute-done.2.refs_1_, f32[1,16,4096]{2,1,0:T(8,128)S(1)} %collective-permute-done.4.refs_2_, f32[1,16,4096]{2,1,0:T(8,128)S(1)} %collective-permute-done.9.refs_3_, ...), custom_call_target="tpu_custom_call" | custom-call | tf_op jit(solution)/shard_map/pallas_call | solution.py:225
  (1 shorter events, 0.0 us)
Async XLA Ops:
  0.0 6.1 %collective-permute-start = (f32[2,16,4096]{2,1,0:T(8,128)}, f32[2,16,4096]{2,1,0:T(8,128)S(1)}, u32[]{:S(2)}, u32[]{:S(2)}) collective-permute-start(f32[2,16,4096]{2,1,0:T(8,128)} %source.1), channel_id=1, source_target_pairs={{1,0},{0,1},{3,2},{2,3},{5,4},{4,5},{7,6},{6,7},{9,8},{8,9},{11,10... | collective-permute-start | bytes 1572872 | tf_op jit(solution)/shard_map/ppermute | solution.py:236
  1.5 9.7 %collective-permute-start.3 = (f32[1,16,4096]{2,1,0:T(8,128)S(1)}, f32[1,16,4096]{2,1,0:T(8,128)S(1)}, u32[]{:S(2)}, u32[]{:S(2)}) collective-permute-start(f32[1,16,4096]{2,1,0:T(8,128)S(1)} %get-tuple-element.21.refs_0_), channel_id=1, source_target_pairs={{2,0},{3,1},{0,2},{1,3},{6,4},{7,5},{4,6},{5,7},{10,8},{11,9},{8,1... | collective-permute-start | bytes 786440 | tf_op jit(solution)/shard_map/ppermute | solution.py:236
  4.1 11.8 %collective-permute-start.10 = (f32[1,16,4096]{2,1,0:T(8,128)S(1)}, f32[1,16,4096]{2,1,0:T(8,128)S(1)}, u32[]{:S(2)}, u32[]{:S(2)}) collective-permute-start(f32[1,16,4096]{2,1,0:T(8,128)S(1)} %get-tuple-element.24.refs_4_), channel_id=1, source_target_pairs={{28,0},{0,4},{4,8},{8,12},{12,16},{16,20},{20,24},{24,28},{29,1},{... | collective-permute-start | bytes 786440 | tf_op jit(solution)/shard_map/ppermute | solution.py:241
  5.6 11.1 %collective-permute-start.6 = (f32[1,16,4096]{2,1,0:T(8,128)S(1)}, f32[1,16,4096]{2,1,0:T(8,128)S(1)}, u32[]{:S(2)}, u32[]{:S(2)}) collective-permute-start(f32[1,16,4096]{2,1,0:T(8,128)S(1)} %get-tuple-element.24.refs_4_), channel_id=1, source_target_pairs={{2,0},{3,1},{0,2},{1,3},{6,4},{7,5},{4,6},{5,7},{10,8},{11,9},{8,1... | collective-permute-start | bytes 786440 | tf_op jit(solution)/shard_map/ppermute | solution.py:236
  6.1 15.4 %collective-permute-start.1 = (f32[1,16,4096]{2,1,0:T(8,128)S(1)}, f32[1,16,4096]{2,1,0:T(8,128)S(1)}, u32[]{:S(2)}, u32[]{:S(2)}) collective-permute-start(f32[1,16,4096]{2,1,0:T(8,128)S(1)} %get-tuple-element.21.refs_0_), channel_id=1, source_target_pairs={{28,0},{0,4},{4,8},{8,12},{12,16},{16,20},{20,24},{24,28},{29,1},{... | collective-permute-start | bytes 786440 | tf_op jit(solution)/shard_map/ppermute | solution.py:241
  11.2 10.3 %collective-permute-start.5 = (f32[1,16,4096]{2,1,0:T(8,128)S(1)}, f32[1,16,4096]{2,1,0:T(8,128)S(1)}, u32[]{:S(2)}, u32[]{:S(2)}) collective-permute-start(f32[1,16,4096]{2,1,0:T(8,128)S(1)} %collective-permute-done.3.refs_2_), channel_id=1, source_target_pairs={{1,0},{0,1},{3,2},{2,3},{5,4},{4,5},{7,6},{6,7},{9,8},{8,9},{11,10... | collective-permute-start | bytes 786440 | tf_op jit(solution)/shard_map/ppermute | solution.py:236
  11.2 16.1 %collective-permute-start.4 = (f32[1,16,4096]{2,1,0:T(8,128)S(1)}, f32[1,16,4096]{2,1,0:T(8,128)S(1)}, u32[]{:S(2)}, u32[]{:S(2)}) collective-permute-start(f32[1,16,4096]{2,1,0:T(8,128)S(1)} %collective-permute-done.3.refs_2_), channel_id=1, source_target_pairs={{28,0},{0,4},{4,8},{8,12},{12,16},{16,20},{20,24},{24,28},{29,1},{... | collective-permute-start | bytes 786440 | tf_op jit(solution)/shard_map/ppermute | solution.py:241
  15.9 11.8 %collective-permute-start.12 = (f32[1,16,4096]{2,1,0:T(8,128)S(1)}, f32[1,16,4096]{2,1,0:T(8,128)S(1)}, u32[]{:S(2)}, u32[]{:S(2)}) collective-permute-start(f32[1,16,4096]{2,1,0:T(8,128)S(1)} %collective-permute-done.10.refs_4_), channel_id=1, source_target_pairs={{2,0},{3,1},{0,2},{1,3},{6,4},{7,5},{4,6},{5,7},{10,8},{11,9},{8,1... | collective-permute-start | bytes 786440 | tf_op jit(solution)/shard_map/ppermute | solution.py:236
  21.5 1.4 %collective-permute-start.8 = (f32[1,8,4096]{2,1,0:T(8,128)S(1)}, f32[1,8,4096]{2,1,0:T(8,128)S(1)}, u32[]{:S(2)}, u32[]{:S(2)}) collective-permute-start(f32[1,8,4096]{2,1,0:T(8,128)S(1)} %get-tuple-element.35), channel_id=1, source_target_pairs={{1,0},{0,1},{3,2},{2,3},{5,4},{4,5},{7,6},{6,7},{9,8},{8,9},{11,10... | collective-permute-start | bytes 393224 | tf_op jit(solution)/shard_map/ppermute | solution.py:236
  21.6 1.5 %collective-permute-start.7 = (f32[1,8,4096]{2,1,0:T(8,128)S(1)}, f32[1,8,4096]{2,1,0:T(8,128)S(1)}, u32[]{:S(2)}, u32[]{:S(2)}) collective-permute-start(f32[1,8,4096]{2,1,0:T(8,128)S(1)} %get-tuple-element.36), channel_id=1, source_target_pairs={{1,0},{0,1},{3,2},{2,3},{5,4},{4,5},{7,6},{6,7},{9,8},{8,9},{11,10... | collective-permute-start | bytes 393224 | tf_op jit(solution)/shard_map/ppermute | solution.py:236
  22.1 5.8 %collective-permute-start.11 = (f32[1,16,4096]{2,1,0:T(8,128)S(1)}, f32[1,16,4096]{2,1,0:T(8,128)S(1)}, u32[]{:S(2)}, u32[]{:S(2)}) collective-permute-start(f32[1,16,4096]{2,1,0:T(8,128)S(1)} %collective-permute-done.10.refs_4_), channel_id=1, source_target_pairs={{1,0},{0,1},{3,2},{2,3},{5,4},{4,5},{7,6},{6,7},{9,8},{8,9},{11,10... | collective-permute-start | bytes 786440 | tf_op jit(solution)/shard_map/ppermute | solution.py:236
  22.9 4.9 %collective-permute-start.2 = (f32[1,16,4096]{2,1,0:T(8,128)S(1)}, f32[1,16,4096]{2,1,0:T(8,128)S(1)}, u32[]{:S(2)}, u32[]{:S(2)}) collective-permute-start(f32[1,16,4096]{2,1,0:T(8,128)S(1)} %collective-permute-done.1.refs_9_.refs_0_), channel_id=1, source_target_pairs={{1,0},{0,1},{3,2},{2,3},{5,4},{4,5},{7,6},{6,7},{9,8},{8,9},{11,10... | collective-permute-start | bytes 786440 | tf_op jit(solution)/shard_map/ppermute | solution.py:236
  27.3 1.6 %collective-permute-start.9 = (f32[1,16,4096]{2,1,0:T(8,128)S(1)}, f32[1,16,4096]{2,1,0:T(8,128)S(1)}, u32[]{:S(2)}, u32[]{:S(2)}) collective-permute-start(f32[1,16,4096]{2,1,0:T(8,128)S(1)} %collective-permute-done.4.refs_2_), channel_id=1, source_target_pairs={{1,0},{0,1},{3,2},{2,3},{5,4},{4,5},{7,6},{6,7},{9,8},{8,9},{11,10... | collective-permute-start | bytes 786440 | tf_op jit(solution)/shard_map/ppermute | solution.py:236
  27.7 1.6 %collective-permute-start.13 = (f32[1,16,4096]{2,1,0:T(8,128)S(1)}, f32[1,16,4096]{2,1,0:T(8,128)S(1)}, u32[]{:S(2)}, u32[]{:S(2)}) collective-permute-start(f32[1,16,4096]{2,1,0:T(8,128)S(1)} %collective-permute-done.12.refs_6_), channel_id=1, source_target_pairs={{1,0},{0,1},{3,2},{2,3},{5,4},{4,5},{7,6},{6,7},{9,8},{8,9},{11,10... | collective-permute-start | bytes 786440 | tf_op jit(solution)/shard_map/ppermute | solution.py:236

commit v2 on v1

--- a/solution.py
+++ b/solution.py
@@ -36,8 +36,12 @@
     pair_low = np.block([[low, none], [none, low]])
     lane_table = np.block([[pair_high, pair_low], [pair_high, pair_low]])
     order = np.concatenate([np.arange(0, cells, 2), np.arange(1, cells, 2)])
-    plane_table = np.stack([np.concatenate([high[:, rows], high[:, rows], low[:, rows]], 1) for rows in layouts])
-    plane_back_table = np.stack([np.concatenate([high[rows], high[rows], low[rows]], 1) for rows in layouts])
+    def across_planes(rows):
+        return np.concatenate([high[:, rows], high[:, rows], low[:, rows]], 1)
+
+    plane_table = np.stack([np.stack([across_planes(rows) for rows in spans]) for spans in layouts])
+    whole = [np.concatenate(spans) for spans in layouts]
+    plane_back_table = np.stack([np.concatenate([high[rows], high[rows], low[rows]], 1) for rows in whole])
     column_table = np.concatenate([high[:, order], high[:, order], low[:, order]], 1)
     back_table = np.concatenate([high[order], high[order], low[order]], 1)
     single = 4.0 * np.sin(np.pi * wave / (2.0 * (cells + 1))) ** 2
@@ -110,19 +114,26 @@
     )(pltpu.with_memory_space_constraint(sources, pltpu.HBM))
 
 
-def solve_kernel(cells, groups, spare, first, last, *refs):
-    sources = len(groups)
+def tile(u):
+    return slice(u * LANES, (u + 1) * LANES)
+
+
+def along_lanes(table, values):
+    high, rest = split(values)
+    product = dot(cat([high, rest], 1), table[...])
+    return product[:, :LANES] + product[:, LANES:]
+
+
+def along_rows(table, values):
+    high, rest = split(values)
+    return dot(table, cat([high, rest, high], 0))
+
+
+def readers(cells, groups, refs):
     pieces = []
     for group in groups:
         pieces.append(refs[:len(group)])
         refs = refs[len(group):]
-    refs = refs[spare:]
-    target, refs = refs[0], refs[1:]
-    if not first:
-        before, refs = refs[0], refs[1:]
-    lane_table, plane_table, plane_back_table, column_table, back_table, inverse, out, planes, columns = refs[:9]
-    pairs = cells // 2
-    plane_pitch, column_pitch = cells + 8, pairs + 8
     me = lax.axis_index("member")
     extent = cells // lax.axis_size("member")
     places = [
@@ -138,35 +149,66 @@
         start = offset if distance is None else (me ^ distance) * extent + offset
         return pl.ds(pl.multiple_of(start, ROWS), ROWS)
 
-    order = 0 if layout[0][0] is None else me
-    low = lax.broadcasted_iota(jnp.int32, (pairs, LANES), 1) < cells
-    every = [(j, u) for j in range(sources) for u in range(pairs)]
-
-    def along_lanes(values):
-        high, rest = split(values)
-        product = dot(cat([high, rest], 1), lane_table[...])
-        return product[:, :LANES] + product[:, LANES:]
-
-    def along_rows(table, values):
-        high, rest = split(values)
-        return dot(table, cat([high, rest, high], 0))
-
-    def tile(u):
-        return slice(u * LANES, (u + 1) * LANES)
-
-    def block(u):
-        return slice(u * cells, (u + 1) * cells)
-
     def piece(j, segment, u):
         number, index, row = places[j][segment]
         return pieces[j][number][index, row:row + ROWS, tile(u)]
 
-    segments = range(len(layout))
+    return rows, piece, range(len(layout)), 0 if layout[0][0] is None else me, refs
+
+
+def forward(target, rows, piece, every, segments, lane_table, plane_table):
     field = [target[rows(segment), tile(u)] * piece(j, segment, u) for j, u in every for segment in segments]
-    field = along_lanes(cat(field, 0))
-    field = along_rows(plane_table[order], cat([field[block(i)] for i in range(len(every))], 1))
+    field = along_lanes(lane_table, cat(field, 0))
+    count = ROWS * len(segments)
+    return along_rows(plane_table, cat([field[i * count:(i + 1) * count] for i in range(len(every))], 1))
+
+
+def begin_kernel(cells, groups, spare, *refs):
+    rows, piece, segments, order, refs = readers(cells, groups, refs)
+    target, lane_table, plane_table, planes = refs[spare:]
+    every = [(j, u) for j in range(len(groups)) for u in range(cells // 2)]
+    field = forward(target, rows, piece, every, segments, lane_table, plane_table[order, 0])
     for i, (j, u) in enumerate(every):
-        planes[j, pl.ds(u * plane_pitch, cells), :] = field[:, tile(i)]
+        planes[j, pl.ds(u * cells, cells), :] = field[:, tile(i)]
+
+
+def begin(target, groups, constants, *earlier):
+    cells = target.shape[0]
+    layout = tuple(tuple(part[1:] for part in group) for group in groups)
+    operands = [part[0] for group in groups for part in group] + list(earlier) + [target] + list(constants[:2])
+    operands = [pltpu.with_memory_space_constraint(operand, pltpu.VMEM) for operand in operands]
+    vmem = pl.BlockSpec(memory_space=pltpu.VMEM)
+    return pl.pallas_call(
+        functools.partial(begin_kernel, cells, layout, len(earlier)),
+        out_shape=pltpu.VMEM((len(groups), cells // 2 * cells, LANES), jnp.float32),
+        in_specs=[vmem] * len(operands),
+        out_specs=vmem,
+        compiler_params=pltpu.CompilerParams(vmem_limit_bytes=24 << 20),
+    )(*operands)
+
+
+def solve_kernel(cells, groups, begun, first, last, *refs):
+    sources = len(groups)
+    rows, piece, segments, order, refs = readers(cells, groups, refs)
+    if begun:
+        ready, refs = refs[0], refs[1:]
+    target, refs = refs[0], refs[1:]
+    if not first:
+        before, refs = refs[0], refs[1:]
+    lane_table, plane_table, plane_back_table, column_table, back_table, inverse, out, planes, columns = refs[:9]
+    pairs = cells // 2
+    plane_pitch, column_pitch = cells + 8, pairs + 8
+    low = lax.broadcasted_iota(jnp.int32, (pairs, LANES), 1) < cells
+    every = [(j, u) for j in range(sources) for u in range(pairs)]
+
+    def block(u):
+        return slice(u * cells, (u + 1) * cells)
+
+    missing = segments[len(segments) // 2:] if begun else segments
+    field = forward(target, rows, piece, every, missing, lane_table, plane_table[order, int(begun)])
+    for i, (j, u) in enumerate(every):
+        part = field[:, tile(i)]
+        planes[j, pl.ds(u * plane_pitch, cells), :] = part + ready[j, block(u), :] if begun else part
 
     turned = []
     for j, u in every:
@@ -190,7 +232,7 @@
         some = [(j, u) for j in range(sources) for u in mine]
         field = cat([columns[j, pl.ds(u, cells, column_pitch), :] for j, u in some], 1)
         field = along_rows(plane_back_table[order], field)
-        field = along_lanes(cat([field[:, tile(i)] for i in range(len(some))], 0))
+        field = along_lanes(lane_table, cat([field[:, tile(i)] for i in range(len(some))], 0))
         result = refs[9] if last else out
         for position, u in enumerate(mine):
             for segment in segments:
@@ -208,12 +250,12 @@
         copy.wait()
 
 
-def solve(target, groups, total, constants, last, *earlier):
+def solve(target, groups, ready, total, constants, last):
     cells, plane = target.shape
     vmem = pl.BlockSpec(memory_space=pltpu.VMEM)
     layout = tuple(tuple(part[1:] for part in group) for group in groups)
     operands = [part[0] for group in groups for part in group]
-    operands += list(earlier) + [target] + ([] if total is None else [total]) + list(constants)
+    operands += ([] if ready is None else [ready]) + [target] + ([] if total is None else [total]) + list(constants)
     operands = [pltpu.with_memory_space_constraint(operand, pltpu.VMEM) for operand in operands]
     shape = (cells, plane)
     scratch = [
@@ -223,7 +265,7 @@
     if last:
         scratch += [pltpu.VMEM(shape, jnp.float32), pltpu.SemaphoreType.DMA((CHUNKS,))]
     return pl.pallas_call(
-        functools.partial(solve_kernel, cells, layout, len(earlier), total is None, last),
+        functools.partial(solve_kernel, cells, layout, ready is not None, total is None, last),
         out_shape=jax.ShapeDtypeStruct(shape, jnp.float32) if last else pltpu.VMEM(shape, jnp.float32),
         in_specs=[vmem] * len(operands),
         out_specs=pl.BlockSpec(memory_space=pltpu.HBM if last else pltpu.VMEM),
@@ -250,7 +292,7 @@
     count, extent = sources.shape[:2]
     members = lax.axis_size("member")
     if members != 4:
-        constants = in_vmem([targets[0]] + [jnp.asarray(table) for table in tables(cells, [np.arange(cells)])])
+        constants = in_vmem([targets[0]] + [jnp.asarray(table) for table in tables(cells, [[np.arange(cells)]])])
         total = None
         slab = sources
         for stop in range(STOPS):
@@ -259,10 +301,12 @@
             whole = lax.all_gather(slab, "member", axis=1, tiled=True)
             for index in range(count):
                 last = stop == STOPS - 1 and index == count - 1
-                total = solve(constants[0], [[(whole, index, None, 0, cells)]], total, constants[1:], last)
+                total = solve(constants[0], [[(whole, index, None, 0, cells)]], None, total, constants[1:], last)
         return total[None]
     member_rows = np.arange(cells).reshape(members, extent)
-    layouts = [np.concatenate([member_rows[i ^ k] for k in range(members)]) for i in range(members)]
+    layouts = [
+        [np.concatenate([member_rows[i ^ k] for k in span]) for span in ((0, 1), (2, 3))] for i in range(members)
+    ]
     everything = [jnp.asarray(table) for table in tables(cells, layouts)]
     mine = in_vmem_parts(sources)
     across, far = [None, None], [None, None]
@@ -272,22 +316,25 @@
     near = from_member(sources, 1)
     far[0] = from_band(after(mine[0], near))
     target, *constants = in_vmem([targets[0]] + everything, near)
-    across[0], far[1] = after(across[0], target), after(far[1], target)
+    ready = begin(target, [[(mine[i], 0, 0, 0, extent), (near, i, 1, 0, extent)] for i in range(2)], constants)
+    across[0], far[1] = after(across[0], ready), after(far[1], ready)
     far_across = [from_band(across[0]), from_member(far[1], 2)]
     half = extent // 2
     across_near = [[from_member(across[0], 1)], None]
-    late = after(across[1], across_near[0][0], far[0])
-    across_near[1] = [from_member(late[:, i * half:(i + 1) * half], 1) for i in range(2)]
+    soon = across[1]
+    late = after(across[1], far[0])
+    across_near[1] = [from_member(soon[:, :half], 1), from_member(late[:, half:], 1)]
     groups = [[(mine[i], 0, 0, 0, extent), (near, i, 1, 0, extent), (across[i], 0, 2, 0, extent)] for i in range(2)]
     groups[0] += [(across_near[0][0], 0, 3, 0, extent)]
     groups[1] += [(across_near[1][i], 0, 3, i * half, half) for i in range(2)]
-    total = solve(target, groups, None, constants, False, far[0])
+    total = solve(target, groups, ready, None, constants, False)
     far_near = [from_member(value, 1) for value in far]
+    ready = begin(target, [[(far[i], 0, 0, 0, extent), (far_near[i], 0, 1, 0, extent)] for i in range(2)], constants, total)
     far_across = [after(value, total) for value in far_across]
     far_across_near = [from_member(value, 1) for value in far_across]
     groups = [[(far[i], 0, 0), (far_near[i], 0, 1), (far_across[i], 0, 2), (far_across_near[i], 0, 3)] for i in range(2)]
     groups = [[part + (0, extent) for part in group] for group in groups]
-    total = solve(target, groups, total, constants, True)
+    total = solve(target, groups, ready, total, constants, True)
     return total[None]
 
 

time: 34.4 us -> 33.1 us (0.962)
  waiting for transfers between devices: 12 us -> 10.1 us
  Pallas kernels: 11.9 us -> 12.5 us
    ppermute x11, waiting for transfers between devices: 4.44 us -> 2.7 us  [from_member(): lax.ppermute(piece, 'member', [(i ^ distance, i) for i in range(lax.axis_...]
    pallas_call x2 -> x4, Pallas kernels: 9.09 us -> 9.67 us  [the longest x2 7.99 us: solve(): pl.pallas_call(functools.partial(solve_kernel, cells, layout, ready is no...]
  transfers between devices with their start and end apart: 14 -> 14, of which waited for: 7 -> 7; matrix products, arithmetic and copies ran while one was open for 0% -> 0% of each run, Pallas kernels for 20% -> 25%
where the time goes in v2:
time: 33.1 us; the launch traced here: 32.9 us
  Pallas kernels  12.5 us (38%)
  starting transfers between devices  10.2 us (31%)
  waiting for transfers between devices  10.1 us (31%)
    pallas_call x2, Pallas kernels, solve(): pl.pallas_call(functools.partial(solve_kernel, cells, layout, ready is no...  7.99 us
    ppermute x3, waiting for transfers between devices, from_band(): lax.ppermute(piece, 'band', [((i - 1) % count, i) for i in range(count)])  7.44 us
    ppermute x11, starting transfers between devices, from_member(): lax.ppermute(piece, 'member', [(i ^ distance, i) for i in range(lax.axis_...  5.19 us
    ppermute x3, starting transfers between devices, from_band(): lax.ppermute(piece, 'band', [((i - 1) % count, i) for i in range(count)])  5.01 us
    ppermute x11, waiting for transfers between devices, from_member(): lax.ppermute(piece, 'member', [(i ^ distance, i) for i in range(lax.axis_...  2.7 us
    pallas_call x1, Pallas kernels, in_vmem(): pl.pallas_call(functools.partial(prepare_kernel, len(arrays)), out_shape=...  1.75 us
    pallas_call x2, Pallas kernels, begin(): pl.pallas_call(functools.partial(begin_kernel, cells, layout, len(earlier...  1.69 us
    pallas_call x1, Pallas kernels, in_vmem_parts(): pl.pallas_call(parts_kernel, out_shape=[pltpu.VMEM((1, extent, plane), so...  1.04 us
  transfers between devices with their start and end apart: 14, of which 7 were waited for; matrix products, arithmetic and copies ran while one was open for 0% of the time, Pallas kernels for 25%

profile of v2, /device:TPU:0, one launch (start us, length us, event | category | flops | bytes accessed | tf_op | source)
XLA Modules:
  0.0 32.9 jit_solution(16995372051550064386)
XLA Ops:
  0.0 0.5 %collective-permute-start = (f32[2,16,4096]{2,1,0:T(8,128)}, f32[2,16,4096]{2,1,0:T(8,128)S(1)}, u32[]{:S(2)}, u32[]{:S(2)}) collective-permute-start(f32[2,16,4096]{2,1,0:T(8,128)} %source.1), channel_id=1, source_target_pairs={{1,0},{0,1},{3,2},{2,3},{5,4},{4,5},{7,6},{6,7},{9,8},{8,9},{11,10... | collective-permute-start | bytes 1572872 | tf_op jit(solution)/shard_map/ppermute | solution.py:278
  0.5 1.0 %shard_map.82 = (f32[1,16,4096]{2,1,0:T(8,128)S(1)}, f32[1,16,4096]{2,1,0:T(8,128)S(1)}) custom-call(f32[2,16,4096]{2,1,0:T(8,128)} %source.1), custom_call_target="tpu_custom_call" | custom-call | tf_op jit(solution)/shard_map/pallas_call | solution.py:107
  1.5 2.6 %collective-permute-start.3 = (f32[1,16,4096]{2,1,0:T(8,128)S(1)}, f32[1,16,4096]{2,1,0:T(8,128)S(1)}, u32[]{:S(2)}, u32[]{:S(2)}) collective-permute-start(f32[1,16,4096]{2,1,0:T(8,128)S(1)} %get-tuple-element.21.refs_0_), channel_id=1, source_target_pairs={{2,0},{3,1},{0,2},{1,3},{6,4},{7,5},{4,6},{5,7},{10,8},{11,9},{8,1... | collective-permute-start | bytes 786440 | tf_op jit(solution)/shard_map/ppermute | solution.py:278
  4.1 1.5 %collective-permute-start.10 = (f32[1,16,4096]{2,1,0:T(8,128)S(1)}, f32[1,16,4096]{2,1,0:T(8,128)S(1)}, u32[]{:S(2)}, u32[]{:S(2)}) collective-permute-start(f32[1,16,4096]{2,1,0:T(8,128)S(1)} %get-tuple-element.22.refs_2_.refs_4_), channel_id=1, source_target_pairs={{28,0},{0,4},{4,8},{8,12},{12,16},{16,20},{20,24},{24,28},{29,1},{... | collective-permute-start | bytes 786440 | tf_op jit(solution)/shard_map/ppermute | solution.py:283
  5.6 0.5 %collective-permute-start.6 = (f32[1,16,4096]{2,1,0:T(8,128)S(1)}, f32[1,16,4096]{2,1,0:T(8,128)S(1)}, u32[]{:S(2)}, u32[]{:S(2)}) collective-permute-start(f32[1,16,4096]{2,1,0:T(8,128)S(1)} %get-tuple-element.22.refs_2_.refs_4_), channel_id=1, source_target_pairs={{2,0},{3,1},{0,2},{1,3},{6,4},{7,5},{4,6},{5,7},{10,8},{11,9},{8,1... | collective-permute-start | bytes 786440 | tf_op jit(solution)/shard_map/ppermute | solution.py:278
  6.1 0.0 collective-permute-done.refs_7_.refs_1_.refs_3_.refs_5_
  6.1 1.5 %collective-permute-start.1 = (f32[1,16,4096]{2,1,0:T(8,128)S(1)}, f32[1,16,4096]{2,1,0:T(8,128)S(1)}, u32[]{:S(2)}, u32[]{:S(2)}) collective-permute-start(f32[1,16,4096]{2,1,0:T(8,128)S(1)} %get-tuple-element.21.refs_0_), channel_id=1, source_target_pairs={{28,0},{0,4},{4,8},{8,12},{12,16},{16,20},{20,24},{24,28},{29,1},{... | collective-permute-start | bytes 786440 | tf_op jit(solution)/shard_map/ppermute | solution.py:283
  7.6 1.8 %shard_map.83 = (f32[64,4096]{1,0:T(8,128)S(1)}, bf16[256,256]{1,0:T(8,128)(2,1)S(1)}, bf16[4,2,64,96]{3,2,1,0:T(8,128)(2,1)S(1)}, bf16[4,64,192]{2,1,0:T(8,128)...) custom-call(f32[64,4096]{1,0:T(8,128)} %bitcast.2, ...), custom_call_target="tpu_custom_call" | custom-call | tf_op jit(solution)/shard_map/pallas_call | solution.py:65
  9.4 0.8 %shard_map.84.refs_9_ = f32[2,2048,128]{2,1,0:T(8,128)S(1)} custom-call(f32[1,16,4096]{2,1,0:T(8,128)S(1)} %get-tuple-element.21.refs_0_, f32[2,16,4096]{2,1,0:T(8,128)S(1)} %collective-permute-done.refs_7_.refs_1_.refs_3_.refs_5_, f32[1,16,4096]{2,1,0:T(8,128)S(1)} %get-tuple-element.22.refs_2_.refs_4_, ...), custom_call_target="tpu_custom_call" | custom-call | tf_op jit(solution)/shard_map/pallas_call | solution.py:181
  10.2 1.0 %collective-permute-done.3.refs_2_ = f32[1,16,4096]{2,1,0:T(8,128)S(1)} collective-permute-done((f32[1,16,4096]{2,1,0:T(8,128)S(1)}, f32[1,16,4096]{2,1,0:T(8,128)S(1)}, u32[]{:S(2)}, u32[]{:S(2)}) %collective-permute-start.3) | collective-permute-done | bytes 262176 | tf_op jit(solution)/shard_map/ppermute | solution.py:278
  11.2 0.0 collective-permute-start.5
  11.2 2.0 %collective-permute-start.4 = (f32[1,16,4096]{2,1,0:T(8,128)S(1)}, f32[1,16,4096]{2,1,0:T(8,128)S(1)}, u32[]{:S(2)}, u32[]{:S(2)}) collective-permute-start(f32[1,16,4096]{2,1,0:T(8,128)S(1)} %collective-permute-done.3.refs_2_), channel_id=1, source_target_pairs={{28,0},{0,4},{4,8},{8,12},{12,16},{16,20},{20,24},{24,28},{29,1},{... | collective-permute-start | bytes 786440 | tf_op jit(solution)/shard_map/ppermute | solution.py:283
  13.2 2.7 %collective-permute-done.10.refs_2_.refs_4_ = f32[1,16,4096]{2,1,0:T(8,128)S(1)} collective-permute-done((f32[1,16,4096]{2,1,0:T(8,128)S(1)}, f32[1,16,4096]{2,1,0:T(8,128)S(1)}, u32[]{:S(2)}, u32[]{:S(2)}) %collective-permute-start.10) | collective-permute-done | bytes 262176 | tf_op jit(solution)/shard_map/ppermute | solution.py:283
  15.9 0.3 %collective-permute-start.12 = (f32[1,16,4096]{2,1,0:T(8,128)S(1)}, f32[1,16,4096]{2,1,0:T(8,128)S(1)}, u32[]{:S(2)}, u32[]{:S(2)}) collective-permute-start(f32[1,16,4096]{2,1,0:T(8,128)S(1)} %collective-permute-done.10.refs_2_.refs_4_), channel_id=1, source_target_pairs={{2,0},{3,1},{0,2},{1,3},{6,4},{7,5},{4,6},{5,7},{10,8},{11,9},{8,1... | collective-permute-start | bytes 786440 | tf_op jit(solution)/shard_map/ppermute | solution.py:278
  16.2 0.4 %collective-permute-done.6.refs_6_ = f32[1,16,4096]{2,1,0:T(8,128)S(1)} collective-permute-done((f32[1,16,4096]{2,1,0:T(8,128)S(1)}, f32[1,16,4096]{2,1,0:T(8,128)S(1)}, u32[]{:S(2)}, u32[]{:S(2)}) %collective-permute-start.6) | collective-permute-done | bytes 262176 | tf_op jit(solution)/shard_map/ppermute | solution.py:278
  16.7 0.1 collective-permute-start.7
  16.7 4.8 %collective-permute-done.1.refs_0_ = f32[1,16,4096]{2,1,0:T(8,128)S(1)} collective-permute-done((f32[1,16,4096]{2,1,0:T(8,128)S(1)}, f32[1,16,4096]{2,1,0:T(8,128)S(1)}, u32[]{:S(2)}, u32[]{:S(2)}) %collective-permute-start.1) | collective-permute-done | bytes 262176 | tf_op jit(solution)/shard_map/ppermute | solution.py:283
  21.5 0.1 collective-permute-start.8
  21.6 0.0 collective-permute-done.7.refs_7_
  21.6 0.5 %collective-permute-start.11 = (f32[1,16,4096]{2,1,0:T(8,128)S(1)}, f32[1,16,4096]{2,1,0:T(8,128)S(1)}, u32[]{:S(2)}, u32[]{:S(2)}) collective-permute-start(f32[1,16,4096]{2,1,0:T(8,128)S(1)} %collective-permute-done.10.refs_2_.refs_4_), channel_id=1, source_target_pairs={{1,0},{0,1},{3,2},{2,3},{5,4},{4,5},{7,6},{6,7},{9,8},{8,9},{11,10... | collective-permute-start | bytes 786440 | tf_op jit(solution)/shard_map/ppermute | solution.py:278
  22.1 0.0 collective-permute-done.5.refs_3_
  22.1 0.1 collective-permute-start.2
  22.2 0.7 %collective-permute-done.8.refs_8_ = f32[1,8,4096]{2,1,0:T(8,128)S(1)} collective-permute-done((f32[1,8,4096]{2,1,0:T(8,128)S(1)}, f32[1,8,4096]{2,1,0:T(8,128)S(1)}, u32[]{:S(2)}, u32[]{:S(2)}) %collective-permute-start.8) | collective-permute-done | bytes 131104 | tf_op jit(solution)/shard_map/ppermute | solution.py:278
  22.9 3.7 %shard_map.85.refs_4_.refs_10_ = f32[64,4096]{1,0:T(8,128)S(1)} custom-call(f32[1,16,4096]{2,1,0:T(8,128)S(1)} %get-tuple-element.21.refs_0_, f32[2,16,4096]{2,1,0:T(8,128)S(1)} %collective-permute-done.refs_7_.refs_1_.refs_3_.refs_5_, f32[1,16,4096]{2,1,0:T(8,128)S(1)} %collective-permute-done.3.refs_2_, f32[1,16,4096]{2,1,0:T(8,128)S(1)} %collective-permute-done.5.refs_3_, ...), custom_call_target="tpu_custom_call" | custom-call | tf_op jit(solution)/shard_map/pallas_call | solution.py:267
  26.6 0.2 collective-permute-start.9
  26.8 0.0 collective-permute-done.12.refs_6_
  26.8 0.4 %collective-permute-start.13 = (f32[1,16,4096]{2,1,0:T(8,128)S(1)}, f32[1,16,4096]{2,1,0:T(8,128)S(1)}, u32[]{:S(2)}, u32[]{:S(2)}) collective-permute-start(f32[1,16,4096]{2,1,0:T(8,128)S(1)} %collective-permute-done.12.refs_6_), channel_id=1, source_target_pairs={{1,0},{0,1},{3,2},{2,3},{5,4},{4,5},{7,6},{6,7},{9,8},{8,9},{11,10... | collective-permute-start | bytes 786440 | tf_op jit(solution)/shard_map/ppermute | solution.py:278
  27.2 0.0 collective-permute-done.11.refs_3_.refs_5_
  27.2 0.8 %shard_map.86.refs_8_ = f32[2,2048,128]{2,1,0:T(8,128)S(1)} custom-call(f32[1,16,4096]{2,1,0:T(8,128)S(1)} %collective-permute-done.1.refs_0_, f32[1,16,4096]{2,1,0:T(8,128)S(1)} %collective-permute-done.2.refs_1_, f32[1,16,4096]{2,1,0:T(8,128)S(1)} %collective-permute-done.10.refs_2_.refs_4_, f32[1,16,4096]{2,1,0:T(8,128)S(1)} %collective-permute-done.11.refs_3_.refs_5_, ...), custom_call_target="tpu_custom_call" | custom-call | tf_op jit(solution)/shard_map/pallas_call | solution.py:181
  28.0 0.2 collective-permute-done.9.refs_3_
  28.2 0.4 %collective-permute-done.13.refs_7_ = f32[1,16,4096]{2,1,0:T(8,128)S(1)} collective-permute-done((f32[1,16,4096]{2,1,0:T(8,128)S(1)}, f32[1,16,4096]{2,1,0:T(8,128)S(1)}, u32[]{:S(2)}, u32[]{:S(2)}) %collective-permute-start.13) | collective-permute-done | bytes 262176 | tf_op jit(solution)/shard_map/ppermute | solution.py:278
  28.6 4.3 %shard_map.87 = f32[64,4096]{1,0:T(8,128)} custom-call(f32[1,16,4096]{2,1,0:T(8,128)S(1)} %collective-permute-done.1.refs_0_, f32[1,16,4096]{2,1,0:T(8,128)S(1)} %collective-permute-done.2.refs_1_, f32[1,16,4096]{2,1,0:T(8,128)S(1)} %collective-permute-done.4.refs_2_, f32[1,16,4096]{2,1,0:T(8,128)S(1)} %collective-permute-done.9.refs_3_, ...), custom_call_target="tpu_custom_call" | custom-call | tf_op jit(solution)/shard_map/pallas_call | solution.py:267
  (4 shorter events, 0.0 us)
Async XLA Ops:
  0.0 6.1 %collective-permute-start = (f32[2,16,4096]{2,1,0:T(8,128)}, f32[2,16,4096]{2,1,0:T(8,128)S(1)}, u32[]{:S(2)}, u32[]{:S(2)}) collective-permute-start(f32[2,16,4096]{2,1,0:T(8,128)} %source.1), channel_id=1, source_target_pairs={{1,0},{0,1},{3,2},{2,3},{5,4},{4,5},{7,6},{6,7},{9,8},{8,9},{11,10... | collective-permute-start | bytes 1572872 | tf_op jit(solution)/shard_map/ppermute | solution.py:278
  1.5 9.7 %collective-permute-start.3 = (f32[1,16,4096]{2,1,0:T(8,128)S(1)}, f32[1,16,4096]{2,1,0:T(8,128)S(1)}, u32[]{:S(2)}, u32[]{:S(2)}) collective-permute-start(f32[1,16,4096]{2,1,0:T(8,128)S(1)} %get-tuple-element.21.refs_0_), channel_id=1, source_target_pairs={{2,0},{3,1},{0,2},{1,3},{6,4},{7,5},{4,6},{5,7},{10,8},{11,9},{8,1... | collective-permute-start | bytes 786440 | tf_op jit(solution)/shard_map/ppermute | solution.py:278
  4.1 11.8 %collective-permute-start.10 = (f32[1,16,4096]{2,1,0:T(8,128)S(1)}, f32[1,16,4096]{2,1,0:T(8,128)S(1)}, u32[]{:S(2)}, u32[]{:S(2)}) collective-permute-start(f32[1,16,4096]{2,1,0:T(8,128)S(1)} %get-tuple-element.22.refs_2_.refs_4_), channel_id=1, source_target_pairs={{28,0},{0,4},{4,8},{8,12},{12,16},{16,20},{20,24},{24,28},{29,1},{... | collective-permute-start | bytes 786440 | tf_op jit(solution)/shard_map/ppermute | solution.py:283
  5.6 11.1 %collective-permute-start.6 = (f32[1,16,4096]{2,1,0:T(8,128)S(1)}, f32[1,16,4096]{2,1,0:T(8,128)S(1)}, u32[]{:S(2)}, u32[]{:S(2)}) collective-permute-start(f32[1,16,4096]{2,1,0:T(8,128)S(1)} %get-tuple-element.22.refs_2_.refs_4_), channel_id=1, source_target_pairs={{2,0},{3,1},{0,2},{1,3},{6,4},{7,5},{4,6},{5,7},{10,8},{11,9},{8,1... | collective-permute-start | bytes 786440 | tf_op jit(solution)/shard_map/ppermute | solution.py:278
  6.1 15.4 %collective-permute-start.1 = (f32[1,16,4096]{2,1,0:T(8,128)S(1)}, f32[1,16,4096]{2,1,0:T(8,128)S(1)}, u32[]{:S(2)}, u32[]{:S(2)}) collective-permute-start(f32[1,16,4096]{2,1,0:T(8,128)S(1)} %get-tuple-element.21.refs_0_), channel_id=1, source_target_pairs={{28,0},{0,4},{4,8},{8,12},{12,16},{16,20},{20,24},{24,28},{29,1},{... | collective-permute-start | bytes 786440 | tf_op jit(solution)/shard_map/ppermute | solution.py:283
  11.2 10.9 %collective-permute-start.5 = (f32[1,16,4096]{2,1,0:T(8,128)S(1)}, f32[1,16,4096]{2,1,0:T(8,128)S(1)}, u32[]{:S(2)}, u32[]{:S(2)}) collective-permute-start(f32[1,16,4096]{2,1,0:T(8,128)S(1)} %collective-permute-done.3.refs_2_), channel_id=1, source_target_pairs={{1,0},{0,1},{3,2},{2,3},{5,4},{4,5},{7,6},{6,7},{9,8},{8,9},{11,10... | collective-permute-start | bytes 786440 | tf_op jit(solution)/shard_map/ppermute | solution.py:278
  11.2 15.4 %collective-permute-start.4 = (f32[1,16,4096]{2,1,0:T(8,128)S(1)}, f32[1,16,4096]{2,1,0:T(8,128)S(1)}, u32[]{:S(2)}, u32[]{:S(2)}) collective-permute-start(f32[1,16,4096]{2,1,0:T(8,128)S(1)} %collective-permute-done.3.refs_2_), channel_id=1, source_target_pairs={{28,0},{0,4},{4,8},{8,12},{12,16},{16,20},{20,24},{24,28},{29,1},{... | collective-permute-start | bytes 786440 | tf_op jit(solution)/shard_map/ppermute | solution.py:283
  15.9 10.9 %collective-permute-start.12 = (f32[1,16,4096]{2,1,0:T(8,128)S(1)}, f32[1,16,4096]{2,1,0:T(8,128)S(1)}, u32[]{:S(2)}, u32[]{:S(2)}) collective-permute-start(f32[1,16,4096]{2,1,0:T(8,128)S(1)} %collective-permute-done.10.refs_2_.refs_4_), channel_id=1, source_target_pairs={{2,0},{3,1},{0,2},{1,3},{6,4},{7,5},{4,6},{5,7},{10,8},{11,9},{8,1... | collective-permute-start | bytes 786440 | tf_op jit(solution)/shard_map/ppermute | solution.py:278
  16.7 4.9 %collective-permute-start.7 = (f32[1,8,4096]{2,1,0:T(8,128)S(1)}, f32[1,8,4096]{2,1,0:T(8,128)S(1)}, u32[]{:S(2)}, u32[]{:S(2)}) collective-permute-start(f32[1,8,4096]{2,1,0:T(8,128)S(1)} %slice.8), channel_id=1, source_target_pairs={{1,0},{0,1},{3,2},{2,3},{5,4},{4,5},{7,6},{6,7},{9,8},{8,9},{11,10... | collective-permute-start | bytes 393224 | tf_op jit(solution)/shard_map/ppermute | solution.py:278
  21.5 1.4 %collective-permute-start.8 = (f32[1,8,4096]{2,1,0:T(8,128)S(1)}, f32[1,8,4096]{2,1,0:T(8,128)S(1)}, u32[]{:S(2)}, u32[]{:S(2)}) collective-permute-start(f32[1,8,4096]{2,1,0:T(8,128)S(1)} %slice.7), channel_id=1, source_target_pairs={{1,0},{0,1},{3,2},{2,3},{5,4},{4,5},{7,6},{6,7},{9,8},{8,9},{11,10... | collective-permute-start | bytes 393224 | tf_op jit(solution)/shard_map/ppermute | solution.py:278
  21.6 5.6 %collective-permute-start.11 = (f32[1,16,4096]{2,1,0:T(8,128)S(1)}, f32[1,16,4096]{2,1,0:T(8,128)S(1)}, u32[]{:S(2)}, u32[]{:S(2)}) collective-permute-start(f32[1,16,4096]{2,1,0:T(8,128)S(1)} %collective-permute-done.10.refs_2_.refs_4_), channel_id=1, source_target_pairs={{1,0},{0,1},{3,2},{2,3},{5,4},{4,5},{7,6},{6,7},{9,8},{8,9},{11,10... | collective-permute-start | bytes 786440 | tf_op jit(solution)/shard_map/ppermute | solution.py:278
  22.1 5.1 %collective-permute-start.2 = (f32[1,16,4096]{2,1,0:T(8,128)S(1)}, f32[1,16,4096]{2,1,0:T(8,128)S(1)}, u32[]{:S(2)}, u32[]{:S(2)}) collective-permute-start(f32[1,16,4096]{2,1,0:T(8,128)S(1)} %collective-permute-done.1.refs_0_), channel_id=1, source_target_pairs={{1,0},{0,1},{3,2},{2,3},{5,4},{4,5},{7,6},{6,7},{9,8},{8,9},{11,10... | collective-permute-start | bytes 786440 | tf_op jit(solution)/shard_map/ppermute | solution.py:278
  26.6 1.6 %collective-permute-start.9 = (f32[1,16,4096]{2,1,0:T(8,128)S(1)}, f32[1,16,4096]{2,1,0:T(8,128)S(1)}, u32[]{:S(2)}, u32[]{:S(2)}) collective-permute-start(f32[1,16,4096]{2,1,0:T(8,128)S(1)} %collective-permute-done.4.refs_2_), channel_id=1, source_target_pairs={{1,0},{0,1},{3,2},{2,3},{5,4},{4,5},{7,6},{6,7},{9,8},{8,9},{11,10... | collective-permute-start | bytes 786440 | tf_op jit(solution)/shard_map/ppermute | solution.py:278
  26.8 1.8 %collective-permute-start.13 = (f32[1,16,4096]{2,1,0:T(8,128)S(1)}, f32[1,16,4096]{2,1,0:T(8,128)S(1)}, u32[]{:S(2)}, u32[]{:S(2)}) collective-permute-start(f32[1,16,4096]{2,1,0:T(8,128)S(1)} %collective-permute-done.12.refs_6_), channel_id=1, source_target_pairs={{1,0},{0,1},{3,2},{2,3},{5,4},{4,5},{7,6},{6,7},{9,8},{8,9},{11,10... | collective-permute-start | bytes 786440 | tf_op jit(solution)/shard_map/ppermute | solution.py:278

commit v3 on v2

--- a/solution.py
+++ b/solution.py
@@ -26,7 +26,7 @@
     return high, low
 
 
-def tables(cells, layouts):
+def tables(cells, layouts, spans):
     wave = np.arange(cells) + 1.0
     sine = np.sin(np.pi * wave[:, None] * wave[None, :] / (cells + 1)).astype(np.float32)
     high = sine.astype(jnp.bfloat16)
@@ -39,8 +39,10 @@
     def across_planes(rows):
         return np.concatenate([high[:, rows], high[:, rows], low[:, rows]], 1)
 
-    plane_table = np.stack([np.stack([across_planes(rows) for rows in spans]) for spans in layouts])
-    whole = [np.concatenate(spans) for spans in layouts]
+    plane_tables = [
+        np.stack([across_planes(np.concatenate([pieces[k] for k in span])) for pieces in layouts]) for span in spans
+    ]
+    whole = [np.concatenate(pieces) for pieces in layouts]
     plane_back_table = np.stack([np.concatenate([high[rows], high[rows], low[rows]], 1) for rows in whole])
     column_table = np.concatenate([high[:, order], high[:, order], low[:, order]], 1)
     back_table = np.concatenate([high[order], high[order], low[order]], 1)
@@ -49,7 +51,7 @@
     inverse = (2.0 / (cells + 1)) ** 3 / eigen
     inverse = inverse.reshape(cells // 2, 2, cells, cells).transpose(0, 2, 1, 3)
     inverse = inverse.reshape(cells * cells // 2, 2 * cells).astype(np.float32)
-    return lane_table, plane_table, plane_back_table, column_table, back_table, inverse
+    return lane_table, plane_back_table, column_table, back_table, inverse, *plane_tables
 
 
 def prepare_kernel(count, *refs):
@@ -163,23 +165,25 @@
     return along_rows(plane_table, cat([field[i * count:(i + 1) * count] for i in range(len(every))], 1))
 
 
-def begin_kernel(cells, groups, spare, *refs):
+def begin_kernel(cells, groups, spare, begun, *refs):
     rows, piece, segments, order, refs = readers(cells, groups, refs)
-    target, lane_table, plane_table, planes = refs[spare:]
+    target, lane_table, plane_table, planes = refs[spare + begun:]
     every = [(j, u) for j in range(len(groups)) for u in range(cells // 2)]
-    field = forward(target, rows, piece, every, segments, lane_table, plane_table[order, 0])
+    field = forward(target, rows, piece, every, segments, lane_table, plane_table[order])
     for i, (j, u) in enumerate(every):
-        planes[j, pl.ds(u * cells, cells), :] = field[:, tile(i)]
-
-
-def begin(target, groups, constants, *earlier):
+        part, here = field[:, tile(i)], pl.ds(u * cells, cells)
+        planes[j, here, :] = part + refs[spare][j, here, :] if begun else part
+
+
+def begin(target, groups, ready, constants, *earlier):
     cells = target.shape[0]
     layout = tuple(tuple(part[1:] for part in group) for group in groups)
-    operands = [part[0] for group in groups for part in group] + list(earlier) + [target] + list(constants[:2])
+    operands = [part[0] for group in groups for part in group] + list(earlier) + ([] if ready is None else [ready])
+    operands += [target] + list(constants)
     operands = [pltpu.with_memory_space_constraint(operand, pltpu.VMEM) for operand in operands]
     vmem = pl.BlockSpec(memory_space=pltpu.VMEM)
     return pl.pallas_call(
-        functools.partial(begin_kernel, cells, layout, len(earlier)),
+        functools.partial(begin_kernel, cells, layout, len(earlier), ready is not None),
         out_shape=pltpu.VMEM((len(groups), cells // 2 * cells, LANES), jnp.float32),
         in_specs=[vmem] * len(operands),
         out_specs=vmem,
@@ -195,7 +199,7 @@
     target, refs = refs[0], refs[1:]
     if not first:
         before, refs = refs[0], refs[1:]
-    lane_table, plane_table, plane_back_table, column_table, back_table, inverse, out, planes, columns = refs[:9]
+    lane_table, plane_back_table, column_table, back_table, inverse, plane_table, out, planes, columns = refs[:9]
     pairs = cells // 2
     plane_pitch, column_pitch = cells + 8, pairs + 8
     low = lax.broadcasted_iota(jnp.int32, (pairs, LANES), 1) < cells
@@ -204,8 +208,7 @@
     def block(u):
         return slice(u * cells, (u + 1) * cells)
 
-    missing = segments[len(segments) // 2:] if begun else segments
-    field = forward(target, rows, piece, every, missing, lane_table, plane_table[order, int(begun)])
+    field = forward(target, rows, piece, every, segments[begun:], lane_table, plane_table[order])
     for i, (j, u) in enumerate(every):
         part = field[:, tile(i)]
         planes[j, pl.ds(u * plane_pitch, cells), :] = part + ready[j, block(u), :] if begun else part
@@ -254,6 +257,8 @@
     cells, plane = target.shape
     vmem = pl.BlockSpec(memory_space=pltpu.VMEM)
     layout = tuple(tuple(part[1:] for part in group) for group in groups)
+    planes = constants[-1].shape[-1] // 3
+    begun = 0 if ready is None else (cells - planes) // ROWS
     operands = [part[0] for group in groups for part in group]
     operands += ([] if ready is None else [ready]) + [target] + ([] if total is None else [total]) + list(constants)
     operands = [pltpu.with_memory_space_constraint(operand, pltpu.VMEM) for operand in operands]
@@ -265,7 +270,7 @@
     if last:
         scratch += [pltpu.VMEM(shape, jnp.float32), pltpu.SemaphoreType.DMA((CHUNKS,))]
     return pl.pallas_call(
-        functools.partial(solve_kernel, cells, layout, ready is not None, total is None, last),
+        functools.partial(solve_kernel, cells, layout, begun, total is None, last),
         out_shape=jax.ShapeDtypeStruct(shape, jnp.float32) if last else pltpu.VMEM(shape, jnp.float32),
         in_specs=[vmem] * len(operands),
         out_specs=pl.BlockSpec(memory_space=pltpu.HBM if last else pltpu.VMEM),
@@ -292,7 +297,7 @@
     count, extent = sources.shape[:2]
     members = lax.axis_size("member")
     if members != 4:
-        constants = in_vmem([targets[0]] + [jnp.asarray(table) for table in tables(cells, [[np.arange(cells)]])])
+        constants = in_vmem([targets[0]] + [jnp.asarray(table) for table in tables(cells, [[np.arange(cells)]], [[0]])])
         total = None
         slab = sources
         for stop in range(STOPS):
@@ -304,10 +309,8 @@
                 total = solve(constants[0], [[(whole, index, None, 0, cells)]], None, total, constants[1:], last)
         return total[None]
     member_rows = np.arange(cells).reshape(members, extent)
-    layouts = [
-        [np.concatenate([member_rows[i ^ k] for k in span]) for span in ((0, 1), (2, 3))] for i in range(members)
-    ]
-    everything = [jnp.asarray(table) for table in tables(cells, layouts)]
+    layouts = [[member_rows[i ^ k] for k in range(members)] for i in range(members)]
+    everything = [jnp.asarray(table) for table in tables(cells, layouts, [(0, 1), (2,), (0, 1, 2), (3,)])]
     mine = in_vmem_parts(sources)
     across, far = [None, None], [None, None]
     across[0] = from_member(mine[0], 2)
@@ -315,25 +318,27 @@
     across[1] = from_member(mine[1], 2)
     near = from_member(sources, 1)
     far[0] = from_band(after(mine[0], near))
-    target, *constants = in_vmem([targets[0]] + everything, near)
-    ready = begin(target, [[(mine[i], 0, 0, 0, extent), (near, i, 1, 0, extent)] for i in range(2)], constants)
+    target, lane_table, *constants, own, other, three, rest = in_vmem([targets[0]] + everything, near)
+    constants = [lane_table, *constants, rest]
+    ready = begin(target, [[(mine[i], 0, 0, 0, extent), (near, i, 1, 0, extent)] for i in range(2)], None, (lane_table, own))
     across[0], far[1] = after(across[0], ready), after(far[1], ready)
     far_across = [from_band(across[0]), from_member(far[1], 2)]
     half = extent // 2
     across_near = [[from_member(across[0], 1)], None]
     soon = across[1]
-    late = after(across[1], far[0])
+    ready = begin(target, [[(across[i], 0, 2, 0, extent)] for i in range(2)], ready, (lane_table, other))
+    late = after(across[1], far[0], ready)
     across_near[1] = [from_member(soon[:, :half], 1), from_member(late[:, half:], 1)]
     groups = [[(mine[i], 0, 0, 0, extent), (near, i, 1, 0, extent), (across[i], 0, 2, 0, extent)] for i in range(2)]
     groups[0] += [(across_near[0][0], 0, 3, 0, extent)]
     groups[1] += [(across_near[1][i], 0, 3, i * half, half) for i in range(2)]
     total = solve(target, groups, ready, None, constants, False)
     far_near = [from_member(value, 1) for value in far]
-    ready = begin(target, [[(far[i], 0, 0, 0, extent), (far_near[i], 0, 1, 0, extent)] for i in range(2)], constants, total)
     far_across = [after(value, total) for value in far_across]
     far_across_near = [from_member(value, 1) for value in far_across]
     groups = [[(far[i], 0, 0), (far_near[i], 0, 1), (far_across[i], 0, 2), (far_across_near[i], 0, 3)] for i in range(2)]
     groups = [[part + (0, extent) for part in group] for group in groups]
+    ready = begin(target, [group[:3] for group in groups], None, (lane_table, three), total)
     total = solve(target, groups, ready, total, constants, True)
     return total[None]
 

time: 33.1 us -> 33.1 us (level)
  Pallas kernels: 12.5 us -> 13.4 us
  waiting for transfers between devices: 10.1 us -> 9.25 us
    pallas_call x2 -> x3, Pallas kernels: 1.69 us -> 2.68 us  [begin(): pl.pallas_call(functools.partial(begin_kernel, cells, layout, len(earlier...]
    ppermute x3, waiting for transfers between devices: 7.44 us -> 6.87 us  [from_band(): lax.ppermute(piece, 'band', [((i - 1) % count, i) for i in range(count)])]
  transfers between devices with their start and end apart: 14 -> 14, of which waited for: 7 -> 7; matrix products, arithmetic and copies ran while one was open for 0% -> 0% of each run, Pallas kernels for 25% -> 27%
where the time goes in v3:
time: 33.1 us; the launch traced here: 32.9 us
  Pallas kernels  13.4 us (40%)
  starting transfers between devices  10.1 us (31%)
  waiting for transfers between devices  9.25 us (28%)
    pallas_call x2, Pallas kernels, solve(): pl.pallas_call(functools.partial(solve_kernel, cells, layout, begun, tota...  7.9 us
    ppermute x3, waiting for transfers between devices, from_band(): lax.ppermute(piece, 'band', [((i - 1) % count, i) for i in range(count)])  6.87 us
    ppermute x11, starting transfers between devices, from_member(): lax.ppermute(piece, 'member', [(i ^ distance, i) for i in range(lax.axis_...  5.12 us
    ppermute x3, starting transfers between devices, from_band(): lax.ppermute(piece, 'band', [((i - 1) % count, i) for i in range(count)])  5.01 us
    pallas_call x3, Pallas kernels, begin(): pl.pallas_call(functools.partial(begin_kernel, cells, layout, len(earlier...  2.68 us
    ppermute x11, waiting for transfers between devices, from_member(): lax.ppermute(piece, 'member', [(i ^ distance, i) for i in range(lax.axis_...  2.38 us
    pallas_call x1, Pallas kernels, in_vmem(): pl.pallas_call(functools.partial(prepare_kernel, len(arrays)), out_shape=...  1.77 us
    pallas_call x1, Pallas kernels, in_vmem_parts(): pl.pallas_call(parts_kernel, out_shape=[pltpu.VMEM((1, extent, plane), so...  1.04 us
  transfers between devices with their start and end apart: 14, of which 7 were waited for; matrix products, arithmetic and copies ran while one was open for 0% of the time, Pallas kernels for 27%

profile of v3, /device:TPU:0, one launch (start us, length us, event | category | flops | bytes accessed | tf_op | source)
XLA Modules:
  0.0 32.9 jit_solution(1473609049948761569)
XLA Ops:
  0.0 0.5 %collective-permute-start = (f32[2,16,4096]{2,1,0:T(8,128)}, f32[2,16,4096]{2,1,0:T(8,128)S(1)}, u32[]{:S(2)}, u32[]{:S(2)}) collective-permute-start(f32[2,16,4096]{2,1,0:T(8,128)} %source.1), channel_id=1, source_target_pairs={{1,0},{0,1},{3,2},{2,3},{5,4},{4,5},{7,6},{6,7},{9,8},{8,9},{11,10... | collective-permute-start | bytes 1572872 | tf_op jit(solution)/shard_map/ppermute | solution.py:283
  0.5 1.0 %shard_map.109 = (f32[1,16,4096]{2,1,0:T(8,128)S(1)}, f32[1,16,4096]{2,1,0:T(8,128)S(1)}) custom-call(f32[2,16,4096]{2,1,0:T(8,128)} %source.1), custom_call_target="tpu_custom_call" | custom-call | tf_op jit(solution)/shard_map/pallas_call | solution.py:109
  1.5 2.6 %collective-permute-start.3 = (f32[1,16,4096]{2,1,0:T(8,128)S(1)}, f32[1,16,4096]{2,1,0:T(8,128)S(1)}, u32[]{:S(2)}, u32[]{:S(2)}) collective-permute-start(f32[1,16,4096]{2,1,0:T(8,128)S(1)} %get-tuple-element.24.refs_0_), channel_id=1, source_target_pairs={{2,0},{3,1},{0,2},{1,3},{6,4},{7,5},{4,6},{5,7},{10,8},{11,9},{8,1... | collective-permute-start | bytes 786440 | tf_op jit(solution)/shard_map/ppermute | solution.py:283
  4.1 1.5 %collective-permute-start.10 = (f32[1,16,4096]{2,1,0:T(8,128)S(1)}, f32[1,16,4096]{2,1,0:T(8,128)S(1)}, u32[]{:S(2)}, u32[]{:S(2)}) collective-permute-start(f32[1,16,4096]{2,1,0:T(8,128)S(1)} %get-tuple-element.25.refs_2_.refs_4_), channel_id=1, source_target_pairs={{28,0},{0,4},{4,8},{8,12},{12,16},{16,20},{20,24},{24,28},{29,1},{... | collective-permute-start | bytes 786440 | tf_op jit(solution)/shard_map/ppermute | solution.py:288
  5.6 0.5 %collective-permute-start.6 = (f32[1,16,4096]{2,1,0:T(8,128)S(1)}, f32[1,16,4096]{2,1,0:T(8,128)S(1)}, u32[]{:S(2)}, u32[]{:S(2)}) collective-permute-start(f32[1,16,4096]{2,1,0:T(8,128)S(1)} %get-tuple-element.25.refs_2_.refs_4_), channel_id=1, source_target_pairs={{2,0},{3,1},{0,2},{1,3},{6,4},{7,5},{4,6},{5,7},{10,8},{11,9},{8,1... | collective-permute-start | bytes 786440 | tf_op jit(solution)/shard_map/ppermute | solution.py:283
  6.1 1.5 %collective-permute-start.1 = (f32[1,16,4096]{2,1,0:T(8,128)S(1)}, f32[1,16,4096]{2,1,0:T(8,128)S(1)}, u32[]{:S(2)}, u32[]{:S(2)}) collective-permute-start(f32[1,16,4096]{2,1,0:T(8,128)S(1)} %get-tuple-element.24.refs_0_), channel_id=1, source_target_pairs={{28,0},{0,4},{4,8},{8,12},{12,16},{16,20},{20,24},{24,28},{29,1},{... | collective-permute-start | bytes 786440 | tf_op jit(solution)/shard_map/ppermute | solution.py:288
  7.6 1.8 %shard_map.110 = (f32[64,4096]{1,0:T(8,128)S(1)}, bf16[256,256]{1,0:T(8,128)(2,1)S(1)}, bf16[4,64,192]{2,1,0:T(8,128)(2,1)S(1)}, bf16[64,192]{1,0:T(8,128)(2,1)S...) custom-call(f32[64,4096]{1,0:T(8,128)} %bitcast.2, ...), custom_call_target="tpu_custom_call" | custom-call | tf_op jit(solution)/shard_map/pallas_call | solution.py:67
  9.4 0.8 %shard_map.111.refs_2_ = f32[2,2048,128]{2,1,0:T(8,128)S(1)} custom-call(f32[1,16,4096]{2,1,0:T(8,128)S(1)} %get-tuple-element.24.refs_0_, f32[2,16,4096]{2,1,0:T(8,128)S(1)} %collective-permute-done.refs_10_.refs_1_.refs_3_.refs_5_, f32[1,16,4096]{2,1,0:T(8,128)S(1)} %get-tuple-element.25.refs_2_.refs_4_, ...), custom_call_target="tpu_custom_call" | custom-call | tf_op jit(solution)/shard_map/pallas_call | solution.py:185
  10.3 1.0 %collective-permute-done.3.refs_0_.refs_2_ = f32[1,16,4096]{2,1,0:T(8,128)S(1)} collective-permute-done((f32[1,16,4096]{2,1,0:T(8,128)S(1)}, f32[1,16,4096]{2,1,0:T(8,128)S(1)}, u32[]{:S(2)}, u32[]{:S(2)}) %collective-permute-start.3) | collective-permute-done | bytes 262176 | tf_op jit(solution)/shard_map/ppermute | solution.py:283
  11.2 2.0 %collective-permute-start.4 = (f32[1,16,4096]{2,1,0:T(8,128)S(1)}, f32[1,16,4096]{2,1,0:T(8,128)S(1)}, u32[]{:S(2)}, u32[]{:S(2)}) collective-permute-start(f32[1,16,4096]{2,1,0:T(8,128)S(1)} %collective-permute-done.3.refs_0_.refs_2_), channel_id=1, source_target_pairs={{28,0},{0,4},{4,8},{8,12},{12,16},{16,20},{20,24},{24,28},{29,1},{... | collective-permute-start | bytes 786440 | tf_op jit(solution)/shard_map/ppermute | solution.py:288
  13.2 2.7 %collective-permute-done.10.refs_3_.refs_4_ = f32[1,16,4096]{2,1,0:T(8,128)S(1)} collective-permute-done((f32[1,16,4096]{2,1,0:T(8,128)S(1)}, f32[1,16,4096]{2,1,0:T(8,128)S(1)}, u32[]{:S(2)}, u32[]{:S(2)}) %collective-permute-start.10) | collective-permute-done | bytes 262176 | tf_op jit(solution)/shard_map/ppermute | solution.py:288
  15.9 0.3 %collective-permute-start.12 = (f32[1,16,4096]{2,1,0:T(8,128)S(1)}, f32[1,16,4096]{2,1,0:T(8,128)S(1)}, u32[]{:S(2)}, u32[]{:S(2)}) collective-permute-start(f32[1,16,4096]{2,1,0:T(8,128)S(1)} %collective-permute-done.10.refs_3_.refs_4_), channel_id=1, source_target_pairs={{2,0},{3,1},{0,2},{1,3},{6,4},{7,5},{4,6},{5,7},{10,8},{11,9},{8,1... | collective-permute-start | bytes 786440 | tf_op jit(solution)/shard_map/ppermute | solution.py:283
  16.2 0.4 %collective-permute-done.6.refs_1_.refs_6_ = f32[1,16,4096]{2,1,0:T(8,128)S(1)} collective-permute-done((f32[1,16,4096]{2,1,0:T(8,128)S(1)}, f32[1,16,4096]{2,1,0:T(8,128)S(1)}, u32[]{:S(2)}, u32[]{:S(2)}) %collective-permute-start.6) | collective-permute-done | bytes 262176 | tf_op jit(solution)/shard_map/ppermute | solution.py:283
  16.7 0.1 collective-permute-start.7
  16.7 0.7 %shard_map.112.refs_9_ = f32[2,2048,128]{2,1,0:T(8,128)S(1)} custom-call(f32[1,16,4096]{2,1,0:T(8,128)S(1)} %collective-permute-done.3.refs_0_.refs_2_, f32[1,16,4096]{2,1,0:T(8,128)S(1)} %collective-permute-done.6.refs_1_.refs_6_, f32[2,2048,128]{2,1,0:T(8,128)S(1)} %shard_map.111.refs_2_, ...), custom_call_target="tpu_custom_call" | custom-call | tf_op jit(solution)/shard_map/pallas_call | solution.py:185
  17.5 4.0 %collective-permute-done.1.refs_0_ = f32[1,16,4096]{2,1,0:T(8,128)S(1)} collective-permute-done((f32[1,16,4096]{2,1,0:T(8,128)S(1)}, f32[1,16,4096]{2,1,0:T(8,128)S(1)}, u32[]{:S(2)}, u32[]{:S(2)}) %collective-permute-start.1) | collective-permute-done | bytes 262176 | tf_op jit(solution)/shard_map/ppermute | solution.py:288
  21.5 0.1 collective-permute-start.8
  21.6 0.0 collective-permute-done.7.refs_7_
  21.6 0.5 %collective-permute-start.11 = (f32[1,16,4096]{2,1,0:T(8,128)S(1)}, f32[1,16,4096]{2,1,0:T(8,128)S(1)}, u32[]{:S(2)}, u32[]{:S(2)}) collective-permute-start(f32[1,16,4096]{2,1,0:T(8,128)S(1)} %collective-permute-done.10.refs_3_.refs_4_), channel_id=1, source_target_pairs={{1,0},{0,1},{3,2},{2,3},{5,4},{4,5},{7,6},{6,7},{9,8},{8,9},{11,10... | collective-permute-start | bytes 786440 | tf_op jit(solution)/shard_map/ppermute | solution.py:283
  22.1 0.0 collective-permute-done.5.refs_3_
  22.1 0.1 collective-permute-start.2
  22.2 0.7 %collective-permute-done.8.refs_8_ = f32[1,8,4096]{2,1,0:T(8,128)S(1)} collective-permute-done((f32[1,8,4096]{2,1,0:T(8,128)S(1)}, f32[1,8,4096]{2,1,0:T(8,128)S(1)}, u32[]{:S(2)}, u32[]{:S(2)}) %collective-permute-start.8) | collective-permute-done | bytes 131104 | tf_op jit(solution)/shard_map/ppermute | solution.py:283
  22.9 3.5 %shard_map.113.refs_6_.refs_10_ = f32[64,4096]{1,0:T(8,128)S(1)} custom-call(f32[1,16,4096]{2,1,0:T(8,128)S(1)} %get-tuple-element.24.refs_0_, f32[2,16,4096]{2,1,0:T(8,128)S(1)} %collective-permute-done.refs_10_.refs_1_.refs_3_.refs_5_, f32[1,16,4096]{2,1,0:T(8,128)S(1)} %collective-permute-done.3.refs_0_.refs_2_, ...), custom_call_target="tpu_custom_call" | custom-call | tf_op jit(solution)/shard_map/pallas_call | solution.py:272
  26.4 0.1 collective-permute-done.4.refs_2_
  26.5 0.1 collective-permute-start.9
  26.6 0.4 %collective-permute-start.13 = (f32[1,16,4096]{2,1,0:T(8,128)S(1)}, f32[1,16,4096]{2,1,0:T(8,128)S(1)}, u32[]{:S(2)}, u32[]{:S(2)}) collective-permute-start(f32[1,16,4096]{2,1,0:T(8,128)S(1)} %collective-permute-done.12.refs_5_.refs_6_), channel_id=1, source_target_pairs={{1,0},{0,1},{3,2},{2,3},{5,4},{4,5},{7,6},{6,7},{9,8},{8,9},{11,10... | collective-permute-start | bytes 786440 | tf_op jit(solution)/shard_map/ppermute | solution.py:283
  27.1 0.0 collective-permute-done.11.refs_4_.refs_5_
  27.1 0.0 collective-permute-done.2.refs_1_
  27.1 1.1 %shard_map.114.refs_8_ = f32[2,2048,128]{2,1,0:T(8,128)S(1)} custom-call(f32[1,16,4096]{2,1,0:T(8,128)S(1)} %collective-permute-done.1.refs_0_, f32[1,16,4096]{2,1,0:T(8,128)S(1)} %collective-permute-done.2.refs_1_, f32[1,16,4096]{2,1,0:T(8,128)S(1)} %collective-permute-done.4.refs_2_, f32[1,16,4096]{2,1,0:T(8,128)S(1)} %collective-permute-done.10.refs_3_.refs_4_, ...), custom_call_target="tpu_custom_call" | custom-call | tf_op jit(solution)/shard_map/pallas_call | solution.py:185
  28.2 0.0 collective-permute-done.9.refs_3_
  28.2 0.2 collective-permute-done.13.refs_7_
  28.5 4.4 %shard_map.115 = f32[64,4096]{1,0:T(8,128)} custom-call(f32[1,16,4096]{2,1,0:T(8,128)S(1)} %collective-permute-done.1.refs_0_, f32[1,16,4096]{2,1,0:T(8,128)S(1)} %collective-permute-done.2.refs_1_, f32[1,16,4096]{2,1,0:T(8,128)S(1)} %collective-permute-done.4.refs_2_, f32[1,16,4096]{2,1,0:T(8,128)S(1)} %collective-permute-done.9.refs_3_, ...), custom_call_target="tpu_custom_call" | custom-call | tf_op jit(solution)/shard_map/pallas_call | solution.py:272
  (5 shorter events, 0.0 us)
Async XLA Ops:
  0.0 6.1 %collective-permute-start = (f32[2,16,4096]{2,1,0:T(8,128)}, f32[2,16,4096]{2,1,0:T(8,128)S(1)}, u32[]{:S(2)}, u32[]{:S(2)}) collective-permute-start(f32[2,16,4096]{2,1,0:T(8,128)} %source.1), channel_id=1, source_target_pairs={{1,0},{0,1},{3,2},{2,3},{5,4},{4,5},{7,6},{6,7},{9,8},{8,9},{11,10... | collective-permute-start | bytes 1572872 | tf_op jit(solution)/shard_map/ppermute | solution.py:283
  1.5 9.7 %collective-permute-start.3 = (f32[1,16,4096]{2,1,0:T(8,128)S(1)}, f32[1,16,4096]{2,1,0:T(8,128)S(1)}, u32[]{:S(2)}, u32[]{:S(2)}) collective-permute-start(f32[1,16,4096]{2,1,0:T(8,128)S(1)} %get-tuple-element.24.refs_0_), channel_id=1, source_target_pairs={{2,0},{3,1},{0,2},{1,3},{6,4},{7,5},{4,6},{5,7},{10,8},{11,9},{8,1... | collective-permute-start | bytes 786440 | tf_op jit(solution)/shard_map/ppermute | solution.py:283
  4.1 11.8 %collective-permute-start.10 = (f32[1,16,4096]{2,1,0:T(8,128)S(1)}, f32[1,16,4096]{2,1,0:T(8,128)S(1)}, u32[]{:S(2)}, u32[]{:S(2)}) collective-permute-start(f32[1,16,4096]{2,1,0:T(8,128)S(1)} %get-tuple-element.25.refs_2_.refs_4_), channel_id=1, source_target_pairs={{28,0},{0,4},{4,8},{8,12},{12,16},{16,20},{20,24},{24,28},{29,1},{... | collective-permute-start | bytes 786440 | tf_op jit(solution)/shard_map/ppermute | solution.py:288
  5.6 11.1 %collective-permute-start.6 = (f32[1,16,4096]{2,1,0:T(8,128)S(1)}, f32[1,16,4096]{2,1,0:T(8,128)S(1)}, u32[]{:S(2)}, u32[]{:S(2)}) collective-permute-start(f32[1,16,4096]{2,1,0:T(8,128)S(1)} %get-tuple-element.25.refs_2_.refs_4_), channel_id=1, source_target_pairs={{2,0},{3,1},{0,2},{1,3},{6,4},{7,5},{4,6},{5,7},{10,8},{11,9},{8,1... | collective-permute-start | bytes 786440 | tf_op jit(solution)/shard_map/ppermute | solution.py:283
  6.1 15.4 %collective-permute-start.1 = (f32[1,16,4096]{2,1,0:T(8,128)S(1)}, f32[1,16,4096]{2,1,0:T(8,128)S(1)}, u32[]{:S(2)}, u32[]{:S(2)}) collective-permute-start(f32[1,16,4096]{2,1,0:T(8,128)S(1)} %get-tuple-element.24.refs_0_), channel_id=1, source_target_pairs={{28,0},{0,4},{4,8},{8,12},{12,16},{16,20},{20,24},{24,28},{29,1},{... | collective-permute-start | bytes 786440 | tf_op jit(solution)/shard_map/ppermute | solution.py:288
  11.2 10.9 %collective-permute-start.5 = (f32[1,16,4096]{2,1,0:T(8,128)S(1)}, f32[1,16,4096]{2,1,0:T(8,128)S(1)}, u32[]{:S(2)}, u32[]{:S(2)}) collective-permute-start(f32[1,16,4096]{2,1,0:T(8,128)S(1)} %collective-permute-done.3.refs_0_.refs_2_), channel_id=1, source_target_pairs={{1,0},{0,1},{3,2},{2,3},{5,4},{4,5},{7,6},{6,7},{9,8},{8,9},{11,10... | collective-permute-start | bytes 786440 | tf_op jit(solution)/shard_map/ppermute | solution.py:283
  11.2 15.3 %collective-permute-start.4 = (f32[1,16,4096]{2,1,0:T(8,128)S(1)}, f32[1,16,4096]{2,1,0:T(8,128)S(1)}, u32[]{:S(2)}, u32[]{:S(2)}) collective-permute-start(f32[1,16,4096]{2,1,0:T(8,128)S(1)} %collective-permute-done.3.refs_0_.refs_2_), channel_id=1, source_target_pairs={{28,0},{0,4},{4,8},{8,12},{12,16},{16,20},{20,24},{24,28},{29,1},{... | collective-permute-start | bytes 786440 | tf_op jit(solution)/shard_map/ppermute | solution.py:288
  15.9 10.7 %collective-permute-start.12 = (f32[1,16,4096]{2,1,0:T(8,128)S(1)}, f32[1,16,4096]{2,1,0:T(8,128)S(1)}, u32[]{:S(2)}, u32[]{:S(2)}) collective-permute-start(f32[1,16,4096]{2,1,0:T(8,128)S(1)} %collective-permute-done.10.refs_3_.refs_4_), channel_id=1, source_target_pairs={{2,0},{3,1},{0,2},{1,3},{6,4},{7,5},{4,6},{5,7},{10,8},{11,9},{8,1... | collective-permute-start | bytes 786440 | tf_op jit(solution)/shard_map/ppermute | solution.py:283
  16.7 4.9 %collective-permute-start.7 = (f32[1,8,4096]{2,1,0:T(8,128)S(1)}, f32[1,8,4096]{2,1,0:T(8,128)S(1)}, u32[]{:S(2)}, u32[]{:S(2)}) collective-permute-start(f32[1,8,4096]{2,1,0:T(8,128)S(1)} %slice.8), channel_id=1, source_target_pairs={{1,0},{0,1},{3,2},{2,3},{5,4},{4,5},{7,6},{6,7},{9,8},{8,9},{11,10... | collective-permute-start | bytes 393224 | tf_op jit(solution)/shard_map/ppermute | solution.py:283
  21.5 1.4 %collective-permute-start.8 = (f32[1,8,4096]{2,1,0:T(8,128)S(1)}, f32[1,8,4096]{2,1,0:T(8,128)S(1)}, u32[]{:S(2)}, u32[]{:S(2)}) collective-permute-start(f32[1,8,4096]{2,1,0:T(8,128)S(1)} %slice.7), channel_id=1, source_target_pairs={{1,0},{0,1},{3,2},{2,3},{5,4},{4,5},{7,6},{6,7},{9,8},{8,9},{11,10... | collective-permute-start | bytes 393224 | tf_op jit(solution)/shard_map/ppermute | solution.py:283
  21.6 5.5 %collective-permute-start.11 = (f32[1,16,4096]{2,1,0:T(8,128)S(1)}, f32[1,16,4096]{2,1,0:T(8,128)S(1)}, u32[]{:S(2)}, u32[]{:S(2)}) collective-permute-start(f32[1,16,4096]{2,1,0:T(8,128)S(1)} %collective-permute-done.10.refs_3_.refs_4_), channel_id=1, source_target_pairs={{1,0},{0,1},{3,2},{2,3},{5,4},{4,5},{7,6},{6,7},{9,8},{8,9},{11,10... | collective-permute-start | bytes 786440 | tf_op jit(solution)/shard_map/ppermute | solution.py:283
  22.1 5.0 %collective-permute-start.2 = (f32[1,16,4096]{2,1,0:T(8,128)S(1)}, f32[1,16,4096]{2,1,0:T(8,128)S(1)}, u32[]{:S(2)}, u32[]{:S(2)}) collective-permute-start(f32[1,16,4096]{2,1,0:T(8,128)S(1)} %collective-permute-done.1.refs_0_), channel_id=1, source_target_pairs={{1,0},{0,1},{3,2},{2,3},{5,4},{4,5},{7,6},{6,7},{9,8},{8,9},{11,10... | collective-permute-start | bytes 786440 | tf_op jit(solution)/shard_map/ppermute | solution.py:283
  26.5 1.7 %collective-permute-start.9 = (f32[1,16,4096]{2,1,0:T(8,128)S(1)}, f32[1,16,4096]{2,1,0:T(8,128)S(1)}, u32[]{:S(2)}, u32[]{:S(2)}) collective-permute-start(f32[1,16,4096]{2,1,0:T(8,128)S(1)} %collective-permute-done.4.refs_2_), channel_id=1, source_target_pairs={{1,0},{0,1},{3,2},{2,3},{5,4},{4,5},{7,6},{6,7},{9,8},{8,9},{11,10... | collective-permute-start | bytes 786440 | tf_op jit(solution)/shard_map/ppermute | solution.py:283
  26.6 1.8 %collective-permute-start.13 = (f32[1,16,4096]{2,1,0:T(8,128)S(1)}, f32[1,16,4096]{2,1,0:T(8,128)S(1)}, u32[]{:S(2)}, u32[]{:S(2)}) collective-permute-start(f32[1,16,4096]{2,1,0:T(8,128)S(1)} %collective-permute-done.12.refs_5_.refs_6_), channel_id=1, source_target_pairs={{1,0},{0,1},{3,2},{2,3},{5,4},{4,5},{7,6},{6,7},{9,8},{8,9},{11,10... | collective-permute-start | bytes 786440 | tf_op jit(solution)/shard_map/ppermute | solution.py:283
